TPU v7x, 32 devices: a whole 2x2x4 slice. The times are simulated.
32 devices in a mesh: wide: 8 (over z, y), tp: 4 (over x, core).
Axes of the slice: x: 2, y: 2, z: 4, core: 2. Of those that a mesh axis runs over, the one named last changes fastest.
Arguments:
- block_input: bfloat16 [16384, 1024], P(('wide', 'tp')), may hold values from -6 to 6
- mix_gain: float32 [1024], replicated, may hold values from 0.5 to 1.5
- query_weight: bfloat16 [1024, 512], P('wide', 'tp'), may hold values from -0.1875 to 0.1875
- zx_weight: bfloat16 [1024, 2, 1536], P('wide', None, 'tp'), may hold values from -0.1875 to 0.1875
- step_weight: bfloat16 [1024, 24], P('wide', 'tp'), may hold values from -0.1875 to 0.1875
- shared_weight: bfloat16 [1024, 4, 128], P('wide'), may hold values from -0.1875 to 0.1875
- conv_inner: float32 [4, 1536], P(None, 'tp'), may hold values from -3 to 3
- conv_shared: float32 [4, 2, 128], replicated, may hold values from -3 to 3
- step_bias: float32 [24], P('tp'), may hold values from -6 to -1
- decay_log: float32 [24], P('tp'), may hold values from 0 to 2.5
- skip_gain: float32 [24], P('tp'), may hold values from 0.5 to 1.5
- attention_out: bfloat16 [512, 1024], P('tp', 'wide'), may hold values from -2 to 2
- mamba_out: bfloat16 [1536, 1024], P('tp', 'wide'), may hold values from -0.3125 to 0.3125
- feed_gain: float32 [1024], replicated, may hold values from 0.5 to 1.5
- gate_up: bfloat16 [1024, 2, 2048], P('wide', None, 'tp'), may hold values from -0.1875 to 0.1875
- down_weight: bfloat16 [2048, 1024], P('tp', 'wide'), may hold values from -0.125 to 0.125
- output_grad: bfloat16 [16384, 1024], P(('wide', 'tp')), may hold values from -6 to 6
Outputs:
- block_output: bfloat16 [16384, 1024], P(('wide', 'tp'))
- input_grad: bfloat16 [16384, 1024], P(('wide', 'tp'))
- mix_gain_grad: float32 [1024], replicated
- query_grad: float32 [1024, 512], P('wide', 'tp')
- zx_grad: float32 [1024, 2, 1536], P('wide', None, 'tp')
- step_grad: float32 [1024, 24], P('wide', 'tp')
- shared_grad: float32 [1024, 4, 128], P('wide')
- conv_inner_grad: float32 [4, 1536], P(None, 'tp')
- conv_shared_grad: float32 [4, 2, 128], replicated
- step_bias_grad: float32 [24], P('tp')
- decay_log_grad: float32 [24], P('tp')
- skip_gain_grad: float32 [24], P('tp')
- attention_out_grad: float32 [512, 1024], P('tp', 'wide')
- mamba_out_grad: float32 [1536, 1024], P('tp', 'wide')
- feed_gain_grad: float32 [1024], replicated
- gate_up_grad: float32 [1024, 2, 2048], P('wide', None, 'tp')
- down_grad: float32 [2048, 1024], P('tp', 'wide')
All inputs are finite; a program needn't handle non-finite values.
Results may differ from a plain program's by a relative error of at most 0.024.
Values may be sent and summed in bfloat16 or wider, within the bound.
A program may use at most 192 MiB of HBM per device.

v0:
```python
from functools import partial

import jax
import jax.numpy as jnp
from jax import lax
from jax.sharding import PartitionSpec as P

HEADS = 8
KV_HEADS = 2
HEAD_DIM = 64
SEQ_LEN = 2048
SPAN = 128
QBLOCK = 512


epsilon = 1e-06
HIGHEST_PRECISION = lax.Precision.HIGHEST


def rms_norm(values, gain):
    factor = lax.rsqrt(jnp.mean(values * values, axis=-1, keepdims=True) + epsilon)
    return values * factor * gain


def causal_conv(signal, kernel):
    taps = kernel.shape[0]
    length = signal.shape[1]
    padded = jnp.pad(signal, ((0, 0), (taps - 1, 0), (0, 0)))
    result = jnp.zeros_like(signal)
    for offset in range(taps):
        result = result + padded[:, offset : offset + length, :] * kernel[offset]
    return result


def ssd_scan(inner_vals, step_sizes, decay_rate, key_rows, query_rows, block):
    seq_count, length, head_count, head_width = inner_vals.shape
    span_count = length // block
    span_inputs = inner_vals.reshape(seq_count, span_count, block, head_count, head_width)
    span_steps = step_sizes.reshape(seq_count, span_count, block, head_count)
    span_keys = key_rows.reshape(seq_count, span_count, block, -1)
    span_queries = query_rows.reshape(seq_count, span_count, block, -1)
    cumulative = jnp.cumsum(span_steps * decay_rate, axis=2)
    affinity = jnp.einsum("scqn,scrn->scqr", span_queries, span_keys, precision=HIGHEST_PRECISION)
    causal = jnp.arange(block)[:, None] >= jnp.arange(block)[None, :]
    spread = cumulative[:, :, :, None, :] - cumulative[:, :, None, :, :]
    within = jnp.exp(jnp.where(causal[None, None, :, :, None], spread, -1e30))
    mixing = affinity[..., None] * within * span_steps[:, :, None, :, :]
    intra = jnp.einsum("scqrh,scrhp->scqhp", mixing, span_inputs, precision=HIGHEST_PRECISION)
    to_end = jnp.exp(cumulative[:, :, -1:, :] - cumulative) * span_steps
    states = jnp.einsum(
        "scqhp,scqn->schpn", span_inputs * to_end[..., None], span_keys, precision=HIGHEST_PRECISION
    )
    totals = jnp.exp(cumulative[:, :, -1, :])

    def advance(carried, element):
        factor, fresh = element
        return (carried * factor[:, :, None, None] + fresh, carried)

    start_state = jnp.zeros((seq_count, head_count, head_width, span_keys.shape[-1]), jnp.float32)
    _, prior = lax.scan(
        advance, start_state, (jnp.moveaxis(totals, 1, 0), jnp.moveaxis(states, 1, 0))
    )
    prior = jnp.moveaxis(prior, 0, 1)
    inter = (
        jnp.einsum("scqn,schpn->scqhp", span_queries, prior, precision=HIGHEST_PRECISION)
        * jnp.exp(cumulative)[..., None]
    )
    return (intra + inter).reshape(seq_count, length, head_count, head_width)


def mamba_mix(
    gate_vals,
    inner_raw,
    shared_raw,
    step_raw,
    conv_inner,
    conv_shared,
    step_bias,
    decay_log,
    skip_gain,
    block,
):
    seq_count, length, channel_count = inner_raw.shape
    head_count = step_raw.shape[-1]
    state_size = shared_raw.shape[-1]
    signal = jnp.concatenate(
        [inner_raw, shared_raw.reshape(seq_count, length, 2 * state_size)], axis=-1
    )
    kernel = jnp.concatenate(
        [conv_inner, conv_shared.reshape(conv_shared.shape[0], 2 * state_size)], axis=-1
    )
    convolved = jax.nn.silu(causal_conv(signal, kernel))
    inner_vals = convolved[..., :channel_count].reshape(
        seq_count, length, head_count, channel_count // head_count
    )
    key_rows = convolved[..., channel_count : channel_count + state_size]
    query_rows = convolved[..., channel_count + state_size :]
    step_sizes = jax.nn.softplus(step_raw + step_bias)
    decay_rate = -jnp.exp(decay_log)
    output = (
        ssd_scan(inner_vals, step_sizes, decay_rate, key_rows, query_rows, block)
        + skip_gain[:, None] * inner_vals
    )
    return output.reshape(seq_count, length, channel_count) * jax.nn.silu(gate_vals)


def visible_mask(block_start):
    query_pos = block_start + jnp.arange(QBLOCK)
    key_pos = jnp.arange(SEQ_LEN)
    return query_pos[:, None] >= key_pos[None, :]


def attend_forward(query_heads, key_heads, value_heads):
    scale = HEAD_DIM ** (-0.5)

    def one_block(block_start):
        query_block = lax.dynamic_slice_in_dim(query_heads, block_start, QBLOCK, 1)
        scores = (
            jnp.einsum("sqhd,skd->shqk", query_block, key_heads, preferred_element_type=jnp.float32)
            * scale
        )
        scores = jnp.where(visible_mask(block_start), scores, -1e30)
        row_max = jnp.max(scores, axis=-1, keepdims=True)
        exponent = jnp.exp(scores - row_max)
        row_total = jnp.sum(exponent, axis=-1, keepdims=True)
        soft_low = (exponent / row_total).astype(jnp.bfloat16)
        output = jnp.einsum(
            "shqk,skd->sqhd", soft_low, value_heads, preferred_element_type=jnp.float32
        )
        return (output, row_max + jnp.log(row_total))

    starts = jnp.arange(SEQ_LEN // QBLOCK) * QBLOCK
    outputs, log_totals = lax.map(one_block, starts)
    seq_count = query_heads.shape[0]
    merged = jnp.moveaxis(outputs, 0, 1).reshape(seq_count, SEQ_LEN, query_heads.shape[2], HEAD_DIM)
    return (merged, log_totals)


def attend_backward(query_heads, key_heads, value_heads, log_totals, attn_grad):
    scale = HEAD_DIM ** (-0.5)

    def one_block(carried, element):
        block_start, log_total = element
        query_block = lax.dynamic_slice_in_dim(query_heads, block_start, QBLOCK, 1)
        grad_block = lax.dynamic_slice_in_dim(attn_grad, block_start, QBLOCK, 1)
        scores = (
            jnp.einsum("sqhd,skd->shqk", query_block, key_heads, preferred_element_type=jnp.float32)
            * scale
        )
        scores = jnp.where(visible_mask(block_start), scores, -1e30)
        soft = jnp.exp(scores - log_total)
        soft_low = soft.astype(jnp.bfloat16)
        soft_grad = jnp.einsum(
            "sqhd,skd->shqk", grad_block, value_heads, preferred_element_type=jnp.float32
        )
        score_grad = (
            soft * (soft_grad - jnp.sum(soft * soft_grad, axis=-1, keepdims=True))
        ).astype(jnp.bfloat16)
        query_grad = (
            jnp.einsum("shqk,skd->sqhd", score_grad, key_heads, preferred_element_type=jnp.float32)
            * scale
        )
        key_grad = (
            carried[0]
            + jnp.einsum(
                "shqk,sqhd->skd", score_grad, query_block, preferred_element_type=jnp.float32
            )
            * scale
        )
        value_grad = carried[1] + jnp.einsum(
            "shqk,sqhd->skd", soft_low, grad_block, preferred_element_type=jnp.float32
        )
        return ((key_grad, value_grad), query_grad)

    starts = jnp.arange(SEQ_LEN // QBLOCK) * QBLOCK
    empty = jnp.zeros(key_heads.shape, jnp.float32)
    (key_grad, value_grad), query_grads = lax.scan(one_block, (empty, empty), (starts, log_totals))
    seq_count = query_heads.shape[0]
    query_grad = jnp.moveaxis(query_grads, 0, 1).reshape(
        seq_count, SEQ_LEN, query_heads.shape[2], HEAD_DIM
    )
    return (query_grad, key_grad, value_grad)


def local(
    block_input,
    mix_gain,
    query_weight,
    zx_weight,
    step_weight,
    shared_weight,
    conv_inner,
    conv_shared,
    step_bias,
    decay_log,
    skip_gain,
    attention_out,
    mamba_out,
    feed_gain,
    gate_up,
    down_weight,
    output_grad,
):
    local_heads = query_weight.shape[1] // HEAD_DIM
    group_size = HEADS // KV_HEADS
    kv_owner = lax.axis_index("tp") * local_heads // group_size
    inputs = block_input.astype(jnp.float32)
    normed, norm_pull = jax.vjp(rms_norm, inputs, mix_gain)
    normed_low = normed.astype(jnp.bfloat16)
    gathered = (
        lax.all_gather(query_weight, "wide", axis=0, tiled=True),
        lax.all_gather(zx_weight, "wide", axis=0, tiled=True),
        lax.all_gather(step_weight, "wide", axis=0, tiled=True),
        lax.all_gather(shared_weight, "wide", axis=0, tiled=True),
        lax.all_gather(attention_out, "wide", axis=1, tiled=True),
        lax.all_gather(mamba_out, "wide", axis=1, tiled=True),
        lax.all_gather(gate_up, "wide", axis=0, tiled=True),
        lax.all_gather(down_weight, "wide", axis=1, tiled=True),
    )
    query_full, zx_full, step_full, shared_full, attn_full, mamba_full, gate_up_full, down_full = (
        gathered
    )
    token_rows = lax.all_gather(normed_low, "tp", axis=0, tiled=True)
    token_count = token_rows.shape[0]
    seq_count = token_count // SEQ_LEN
    model_width = token_rows.shape[1]
    query_low = jnp.dot(token_rows, query_full, preferred_element_type=jnp.float32).astype(
        jnp.bfloat16
    )
    kv_weight = lax.dynamic_slice_in_dim(shared_full[:, 0:2, :], kv_owner * HEAD_DIM, HEAD_DIM, 2)
    keyval_low = jnp.einsum(
        "td,dkc->tkc", token_rows, kv_weight, preferred_element_type=jnp.float32
    ).astype(jnp.bfloat16)
    bc_weight = shared_full[:, 2:4, :]
    bc_raw = jnp.einsum("td,dkc->tkc", token_rows, bc_weight, preferred_element_type=jnp.float32)
    gate_input = jnp.einsum("td,dkc->tkc", token_rows, zx_full, preferred_element_type=jnp.float32)
    step_raw = jnp.dot(token_rows, step_full, preferred_element_type=jnp.float32)
    query_heads = query_low.reshape(seq_count, SEQ_LEN, local_heads, HEAD_DIM)
    key_heads = keyval_low[:, 0].reshape(seq_count, SEQ_LEN, HEAD_DIM)
    value_heads = keyval_low[:, 1].reshape(seq_count, SEQ_LEN, HEAD_DIM)
    attn_heads, log_totals = attend_forward(query_heads, key_heads, value_heads)
    attn_low = attn_heads.reshape(token_count, local_heads * HEAD_DIM).astype(jnp.bfloat16)
    channel_count = zx_full.shape[2]
    mamba_local = partial(mamba_mix, block=SPAN)
    gated, mamba_pull = jax.vjp(
        mamba_local,
        gate_input[:, 0].reshape(seq_count, SEQ_LEN, channel_count),
        gate_input[:, 1].reshape(seq_count, SEQ_LEN, channel_count),
        bc_raw.reshape(seq_count, SEQ_LEN, 2, bc_raw.shape[2]),
        step_raw.reshape(seq_count, SEQ_LEN, step_raw.shape[1]),
        conv_inner,
        conv_shared,
        step_bias,
        decay_log,
        skip_gain,
    )
    gated_low = gated.reshape(token_count, channel_count).astype(jnp.bfloat16)
    partial_mix = jnp.dot(attn_low, attn_full, preferred_element_type=jnp.float32) + jnp.dot(
        gated_low, mamba_full, preferred_element_type=jnp.float32
    )
    mixed = lax.psum_scatter(
        partial_mix.astype(jnp.bfloat16), "tp", scatter_dimension=0, tiled=True
    ).astype(jnp.float32)
    hidden_state = inputs + mixed
    normed_two, norm_two_pull = jax.vjp(rms_norm, hidden_state, feed_gain)
    normed_two_low = normed_two.astype(jnp.bfloat16)
    feed_rows = lax.all_gather(normed_two_low, "tp", axis=0, tiled=True)
    gate_up_use, down_use = (gate_up_full, down_full)
    gate_vals = jnp.einsum(
        "td,dkf->tkf", feed_rows, gate_up_use, preferred_element_type=jnp.float32
    )
    gate_part = gate_vals[:, 0]
    up_part = gate_vals[:, 1]
    sigmoid_gate = jax.nn.sigmoid(gate_part)
    silu_gate = gate_part * sigmoid_gate
    hidden_low = (silu_gate * up_part).astype(jnp.bfloat16)
    feed_part = jnp.dot(hidden_low, down_use, preferred_element_type=jnp.float32)
    feed_out = lax.psum_scatter(
        feed_part.astype(jnp.bfloat16), "tp", scatter_dimension=0, tiled=True
    ).astype(jnp.float32)
    block_output = (hidden_state + feed_out).astype(jnp.bfloat16)
    grad_rows = lax.all_gather(output_grad, "tp", axis=0, tiled=True)
    hidden_grad = jnp.einsum("td,fd->tf", grad_rows, down_use, preferred_element_type=jnp.float32)
    down_term = jnp.einsum("tf,td->fd", hidden_low, grad_rows, preferred_element_type=jnp.float32)
    gate_grad = hidden_grad * up_part * (sigmoid_gate * (1.0 + gate_part * (1.0 - sigmoid_gate)))
    up_grad = hidden_grad * silu_gate
    gate_up_low = jnp.stack([gate_grad, up_grad], axis=1).astype(jnp.bfloat16)
    gate_up_term = jnp.einsum(
        "td,tkf->dkf", feed_rows, gate_up_low, preferred_element_type=jnp.float32
    )
    feed_row_grad = jnp.einsum(
        "tkf,dkf->td", gate_up_low, gate_up_use, preferred_element_type=jnp.float32
    )
    normed_two_grad = lax.psum_scatter(
        feed_row_grad.astype(jnp.bfloat16), "tp", scatter_dimension=0, tiled=True
    ).astype(jnp.float32)
    normed_two_grad = normed_two_grad.astype(jnp.bfloat16).astype(jnp.float32)
    state_from_norm, feed_gain_term = norm_two_pull(normed_two_grad)
    state_grad = output_grad.astype(jnp.float32) + state_from_norm
    mixed_rows = lax.all_gather(state_grad.astype(jnp.bfloat16), "tp", axis=0, tiled=True)
    attn_out_term = jnp.einsum(
        "tc,td->cd", attn_low, mixed_rows, preferred_element_type=jnp.float32
    )
    mamba_out_term = jnp.einsum(
        "tc,td->cd", gated_low, mixed_rows, preferred_element_type=jnp.float32
    )
    attn_grad = jnp.einsum(
        "td,cd->tc", mixed_rows, attn_full, preferred_element_type=jnp.float32
    ).astype(jnp.bfloat16)
    gated_grad = (
        jnp.einsum("td,cd->tc", mixed_rows, mamba_full, preferred_element_type=jnp.float32)
        .astype(jnp.bfloat16)
        .astype(jnp.float32)
    )
    mamba_grads = mamba_pull(gated_grad.reshape(seq_count, SEQ_LEN, channel_count))
    (
        gate_in_grad,
        inner_in_grad,
        bc_in_grad,
        step_in_grad,
        conv_inner_term,
        conv_shared_term,
        step_bias_term,
        decay_log_term,
        skip_term,
    ) = mamba_grads
    query_grad, key_grad, value_grad = attend_backward(
        query_heads,
        key_heads,
        value_heads,
        log_totals,
        attn_grad.reshape(seq_count, SEQ_LEN, local_heads, HEAD_DIM),
    )
    query_grad_low = query_grad.reshape(token_count, local_heads * HEAD_DIM).astype(jnp.bfloat16)
    keyval_grad_low = jnp.stack(
        [key_grad.reshape(token_count, HEAD_DIM), value_grad.reshape(token_count, HEAD_DIM)], axis=1
    ).astype(jnp.bfloat16)
    zx_grad_low = jnp.stack(
        [
            gate_in_grad.reshape(token_count, channel_count),
            inner_in_grad.reshape(token_count, channel_count),
        ],
        axis=1,
    ).astype(jnp.bfloat16)
    bc_grad_low = bc_in_grad.reshape(token_count, 2, bc_raw.shape[2]).astype(jnp.bfloat16)
    step_grad_low = step_in_grad.reshape(token_count, step_raw.shape[1]).astype(jnp.bfloat16)
    query_term = jnp.einsum(
        "td,tc->dc", token_rows, query_grad_low, preferred_element_type=jnp.float32
    )
    zx_term = jnp.einsum("td,tkc->dkc", token_rows, zx_grad_low, preferred_element_type=jnp.float32)
    step_term = jnp.einsum(
        "td,th->dh", token_rows, step_grad_low, preferred_element_type=jnp.float32
    )
    keyval_term = jnp.einsum(
        "td,tkc->dkc", token_rows, keyval_grad_low, preferred_element_type=jnp.float32
    )
    bc_term = jnp.einsum("td,tkc->dkc", token_rows, bc_grad_low, preferred_element_type=jnp.float32)
    keyval_placed = lax.dynamic_update_slice_in_dim(
        jnp.zeros((model_width, 2, bc_raw.shape[2]), jnp.float32),
        keyval_term,
        kv_owner * HEAD_DIM,
        2,
    )
    shared_term = jnp.concatenate([keyval_placed, bc_term], axis=1)
    row_grad = jnp.einsum(
        "tc,dc->td", query_grad_low, query_full, preferred_element_type=jnp.float32
    )
    row_grad = row_grad + jnp.einsum(
        "tkc,dkc->td", keyval_grad_low, kv_weight, preferred_element_type=jnp.float32
    )
    row_grad = row_grad + jnp.einsum(
        "tkc,dkc->td", zx_grad_low, zx_full, preferred_element_type=jnp.float32
    )
    row_grad = row_grad + jnp.einsum(
        "tkc,dkc->td", bc_grad_low, bc_weight, preferred_element_type=jnp.float32
    )
    row_grad = row_grad + jnp.einsum(
        "th,dh->td", step_grad_low, step_full, preferred_element_type=jnp.float32
    )
    normed_grad = lax.psum_scatter(
        row_grad.astype(jnp.bfloat16), "tp", scatter_dimension=0, tiled=True
    ).astype(jnp.float32)
    input_from_norm, mix_gain_term = norm_pull(normed_grad)
    input_grad = (state_grad + input_from_norm).astype(jnp.bfloat16)
    summed = (
        lax.psum_scatter(
            query_term.astype(jnp.bfloat16), "wide", scatter_dimension=0, tiled=True
        ).astype(jnp.float32),
        lax.psum_scatter(
            zx_term.astype(jnp.bfloat16), "wide", scatter_dimension=0, tiled=True
        ).astype(jnp.float32),
        lax.psum_scatter(
            step_term.astype(jnp.bfloat16), "wide", scatter_dimension=0, tiled=True
        ).astype(jnp.float32),
        lax.psum_scatter(
            shared_term.astype(jnp.bfloat16), "wide", scatter_dimension=0, tiled=True
        ).astype(jnp.float32),
        lax.psum_scatter(
            attn_out_term.astype(jnp.bfloat16), "wide", scatter_dimension=1, tiled=True
        ).astype(jnp.float32),
        lax.psum_scatter(
            mamba_out_term.astype(jnp.bfloat16), "wide", scatter_dimension=1, tiled=True
        ).astype(jnp.float32),
        lax.psum_scatter(
            gate_up_term.astype(jnp.bfloat16), "wide", scatter_dimension=0, tiled=True
        ).astype(jnp.float32),
        lax.psum_scatter(
            down_term.astype(jnp.bfloat16), "wide", scatter_dimension=1, tiled=True
        ).astype(jnp.float32),
    )
    query_sum, zx_sum, step_sum, shared_part, attn_out_sum, mamba_out_sum, gate_up_sum, down_sum = (
        summed
    )
    small_sums = lax.psum(
        (
            conv_inner_term,
            step_bias_term,
            decay_log_term,
            skip_term,
            mix_gain_term,
            feed_gain_term,
            conv_shared_term,
        ),
        "wide",
    )
    (
        conv_inner_sum,
        step_bias_sum,
        decay_log_sum,
        skip_sum,
        mix_gain_part,
        feed_gain_part,
        conv_shared_part,
    ) = small_sums
    shared_sum, mix_gain_sum, feed_gain_sum, conv_shared_sum = (
        lax.psum(shared_part.astype(jnp.bfloat16), "tp").astype(jnp.float32),
        lax.psum(mix_gain_part.astype(jnp.bfloat16), "tp").astype(jnp.float32),
        lax.psum(feed_gain_part.astype(jnp.bfloat16), "tp").astype(jnp.float32),
        lax.psum(conv_shared_part.astype(jnp.bfloat16), "tp").astype(jnp.float32),
    )
    return (
        block_output,
        input_grad,
        mix_gain_sum,
        query_sum,
        zx_sum,
        step_sum,
        shared_sum,
        conv_inner_sum,
        conv_shared_sum,
        step_bias_sum,
        decay_log_sum,
        skip_sum,
        attn_out_sum,
        mamba_out_sum,
        feed_gain_sum,
        gate_up_sum,
        down_sum,
    )


def solution(mesh):
    placed = (
        P(("wide", "tp"), None),
        P(),
        P("wide", "tp"),
        P("wide", None, "tp"),
        P("wide", "tp"),
        P("wide", None, None),
        P(None, "tp"),
        P(),
        P("tp"),
        P("tp"),
        P("tp"),
        P("tp", "wide"),
        P("tp", "wide"),
        P(),
        P("wide", None, "tp"),
        P("tp", "wide"),
        P(("wide", "tp"), None),
    )
    return jax.shard_map(
        local,
        mesh=mesh,
        in_specs=placed,
        out_specs=(
            P(("wide", "tp"), None),
            P(("wide", "tp"), None),
            P(),
            P("wide", "tp"),
            P("wide", None, "tp"),
            P("wide", "tp"),
            P("wide", None, None),
            P(None, "tp"),
            P(),
            P("tp"),
            P("tp"),
            P("tp"),
            P("tp", "wide"),
            P("tp", "wide"),
            P(),
            P("wide", None, "tp"),
            P("tp", "wide"),
        ),
        check_vma=False,
    )
```

profile of v0, /device:TPU:0, one launch (start us, length us, event | category | flops | bytes accessed | tf_op | source)
XLA Modules:
  0.0 1604.0 jit_solution(10823027199391607262)
XLA Ops:
  14.3 27.8 %all_gather.41 = bf16[1024,6]{0,1:T(8,128)(2,1)S(1)} all-gather(bf16[128,6]{0,1:T(8,128)(2,1)S(1)} %copy-done.135), channel_id=1, replica_groups=mesh['wide'=8,'tp'=4] {'wide'}, dimensions={0}, use_global_device_ids=true | all-gather | bytes 13824 | tf_op jit(solution)/shard_map/all_gather | solution.py:213
  43.4 33.0 %all_gather.37 = bf16[1024,128]{1,0:T(8,128)(2,1)} all-gather(bf16[128,128]{1,0:T(8,128)(2,1)S(1)} %copy-done.111), channel_id=1, replica_groups=mesh['wide'=8,'tp'=4] {'wide'}, dimensions={0}, use_global_device_ids=true | all-gather | bytes 294912 | tf_op jit(solution)/shard_map/all_gather | solution.py:211
  76.3 27.9 %all_gather.39 = bf16[128,1024]{1,0:T(8,128)(2,1)} all-gather(bf16[128,128]{1,0:T(8,128)(2,1)S(1)} %copy-done.112), channel_id=1, replica_groups=mesh['wide'=8,'tp'=4] {'wide'}, dimensions={1}, use_global_device_ids=true | all-gather | bytes 294912 | tf_op jit(solution)/shard_map/all_gather | solution.py:215
  104.3 32.6 %all_gather.42 = bf16[384,1024]{1,0:T(8,128)(2,1)} all-gather(bf16[384,128]{1,0:T(8,128)(2,1)S(1)} %copy-done.88), channel_id=1, replica_groups=mesh['wide'=8,'tp'=4] {'wide'}, dimensions={1}, use_global_device_ids=true | all-gather | bytes 884736 | tf_op jit(solution)/shard_map/all_gather | solution.py:216
  144.3 5.6 fusion.78
  177.3 51.3 %while.61 = (s32[]{:T(128)}, bf16[4,1,512,2,64]{2,4,3,1,0:T(8,128)(2,1)}, f32[4,1,2,512,1]{3,2,4,1,0:T(2,128)S(1)}, s32[4]{0:T(128)S(1)}, bf16[1,2048,2,64]{1,3,...) while((s32[]{:T(128)}, ...), condition=%wide.region_4.5_spmd, body=%wide.region_1.4_spmd.sunk | while | flops 563084800 | bytes 35557628 | solution.py:133
  243.7 72.0 %while.62 = (s32[]{:T(128)}, f32[1,6,64,128]{3,2,1,0:T(8,128)}, f32[16,1,6,64,128]{4,3,2,1,0:T(8,128)S(1)}, f32[16,1,6,1,1]{2,4,3,1,0:T(1,128)}, f32[16,1,6]{2,1...) while((s32[]{:T(128)}, f32[1,6,64,128]{3,2,1,0:T(8,128)}, ...), condition=%wide.region_7.8_spmd.clone, body=%wide.region_6.7_spmd.clone.sunk | while | flops 196611 | bytes 984256 | solution.py:60
  325.5 13.5 bitcast_add_fusion.6
  342.5 8.7 copy.303
  363.6 43.0 %reduce-scatter.21.cloned.1.call-done = bf16[512,1024]{1,0:T(8,128)(2,1)} async-done(((bf16[2048,1024]{1,0:T(8,128)(2,1)}), bf16[512,1024]{1,0:T(8,128)(2,1)}) %reduce-scatter.21.cloned.1.call-update) | async-done | bytes 1048592 | tf_op jit(solution)/shard_map/reduce_scatter | solution.py:261
  412.6 46.1 %all-gather.17.cloned.1.call-done = bf16[1024,2,512]{2,0,1:T(8,128)(2,1)} async-done(((bf16[128,2,512]{2,0,1:T(8,128)(2,1)}), bf16[1024,2,512]{2,0,1:T(8,128)(2,1)}) %all-gather.17.cloned.1.call-update) | async-done | bytes 2097168 | tf_op jit(solution)/shard_map/all_gather | solution.py:217
  458.8 34.5 %all-gather.15.cloned.1.call-done = bf16[2048,1024]{1,0:T(8,128)(2,1)} async-done(((bf16[512,1024]{1,0:T(8,128)(2,1)}), bf16[2048,1024]{1,0:T(8,128)(2,1)}) %all-gather.15.cloned.1.call-update) | async-done | bytes 4194320 | tf_op jit(solution)/shard_map/all_gather | solution.py:267
  493.3 10.7 fusion.72
  504.0 31.1 %all-gather.19.cloned.1.call-done = bf16[512,1024]{1,0:T(8,128)(2,1)} async-done(((bf16[512,128]{1,0:T(8,128)(2,1)}), bf16[512,1024]{1,0:T(8,128)(2,1)}) %all-gather.19.cloned.1.call-update) | async-done | bytes 1048592 | tf_op jit(solution)/shard_map/all_gather | solution.py:218
  535.1 35.0 %all-gather.21.cloned.1.call-done = bf16[2048,1024]{1,0:T(8,128)(2,1)} async-done(((bf16[512,1024]{1,0:T(8,128)(2,1)}), bf16[2048,1024]{1,0:T(8,128)(2,1)}) %all-gather.21.cloned.1.call-update) | async-done | bytes 4194320 | tf_op jit(solution)/shard_map/all_gather | solution.py:282
  570.1 10.4 fusion.140
  582.6 6.3 bitcast_convert_fusion
  589.0 44.7 %reduce-scatter.25.cloned.1.call-done = bf16[512,1024]{1,0:T(8,128)(2,1)} async-done(((bf16[2048,1024]{1,0:T(8,128)(2,1)}), bf16[512,1024]{1,0:T(8,128)(2,1)}) %reduce-scatter.25.cloned.1.call-update) | async-done | bytes 1048592 | tf_op jit(solution)/shard_map/reduce_scatter | solution.py:294
  641.2 8.7 copy.326
  655.4 19.3 %all-gather.23.cloned.1.call-done = bf16[2048,1024]{1,0:T(8,128)(2,1)} async-done(((bf16[512,1024]{1,0:T(8,128)(2,1)}), bf16[2048,1024]{1,0:T(8,128)(2,1)}) %all-gather.23.cloned.1.call-update) | async-done | bytes 4194320 | tf_op jit(solution)/shard_map/all_gather | solution.py:300
  674.7 9.0 fusion.86
  689.4 7.0 fusion.165
  704.9 80.8 %while.63 = (s32[]{:T(128)}, f32[1,2048,64]{1,2,0:T(8,128)}, f32[1,2048,64]{1,2,0:T(8,128)}, bf16[4,1,512,2,64]{2,4,3,1,0:T(8,128)(2,1)}, s32[4]{0:T(128)S(1)}, ...) while((s32[]{:T(128)}, f32[1,2048,64]{1,2,0:T(8,128)}, ...), condition=%wide.region_15.16_spmd.clone, body=%wide.region_13.15_spmd.clone.sunk | while | flops 1375403520 | bytes 82346360 | solution.py:177
  793.7 18.0 %fusion.82 = (f32[16,128,6]{1,2,0:T(8,128)}, f32[16,128,6]{1,2,0:T(8,128)S(1)}, f32[16,128,6]{1,2,0:T(8,128)}, f32[16,128,128]{2,1,0:T(8,128)S(1)}) fusion(f32[16,128,128]{2,1,0:T(8,128)} %copy-done.71, f32[16,128,6]{1,2,0:T(8,128)S(1)} %copy-done.94, f32[16,128,6]{1,2,0:T(8,128)S(1)} %copy-done.92, pred[128,128]{1,0:T(8,128)(4,1)S(1)} %copy-done.124, ...), kind=kOutput, calls=%fused_computation.134 | convolution fusion | flops 1228107776 | bytes 8650752 | tf_op jit(solution)/shard_map/transpose(jvp(scqrh,scrhp->scqhp))/dot_general | solution.py:48
  818.9 40.5 %while.64 = (s32[]{:T(128)}, f32[1,6,64,128]{3,2,1,0:T(8,128)S(1)}, f32[16,1,6]{2,1,0:T(1,128)S(1)}, f32[16,1,6,64,128]{4,3,2,1,0:T(8,128)}, f32[16,1,6,64,128]{...) while((s32[]{:T(128)}, f32[1,6,64,128]{3,2,1,0:T(8,128)S(1)}, ...), condition=%wide.region_19.20_spmd.clone, body=%wide.region_17.19_spmd.clone.sunk | while | flops 294910 | bytes 1180916 | solution.py:60
  859.4 10.3 fusion.173
  873.5 8.0 bitcast_add_fusion.5
  889.9 8.2 fusion.161
  898.6 14.0 multiply_reduce_fusion.3
  912.6 9.8 broadcast_multiply_fusion
  940.8 6.1 convolution_convert_fusion.4
  949.3 9.3 fusion.146
  968.9 5.5 fusion.181
  994.3 8.1 add_convert_fusion.1
  1005.6 7.5 fusion.153
  1023.8 5.8 fusion.141
  1029.6 11.8 fusion.63
  1047.8 24.0 %reduce-scatter.43.cloned.1.call-done = bf16[128,512]{1,0:T(8,128)(2,1)} async-done(((bf16[1024,512]{1,0:T(8,128)(2,1)}), bf16[128,512]{1,0:T(8,128)(2,1)}) %reduce-scatter.43.cloned.1.call-update) | async-done | bytes 131088
  1073.5 68.4 %reduce-scatter.35.cloned.1.call-done = bf16[128,2,512]{2,0,1:T(8,128)(2,1)} async-done(((bf16[1024,2,512]{2,0,1:T(8,128)(2,1)}), bf16[128,2,512]{2,0,1:T(8,128)(2,1)}) %reduce-scatter.35.cloned.1.call-update) | async-done | bytes 262160 | tf_op jit(solution)/shard_map/reduce_scatter | solution.py:404
  1144.3 61.2 %reduce-scatter.37.cloned.1.call-done = bf16[128,6]{1,0:T(8,128)(2,1)} async-done(((bf16[1024,6]{1,0:T(8,128)(2,1)}), bf16[128,6]{1,0:T(8,128)(2,1)}) %reduce-scatter.37.cloned.1.call-update) | async-done | bytes 1552
  1206.9 62.0 %reduce-scatter.39.cloned.1.call-done = bf16[128,128]{1,0:T(8,128)(2,1)} async-done(((bf16[1024,128]{1,0:T(8,128)(2,1)}), bf16[128,128]{1,0:T(8,128)(2,1)}) %reduce-scatter.39.cloned.1.call-update) | async-done | bytes 32784
  1270.4 61.9 %reduce-scatter.29.cloned.1.call-done = bf16[128,128]{1,0:T(8,128)(2,1)} async-done(((bf16[1024,128]{1,0:T(8,128)(2,1)}), bf16[128,128]{1,0:T(8,128)(2,1)}) %reduce-scatter.29.cloned.1.call-update) | async-done | bytes 32784 | tf_op jit(solution)/shard_map/reduce_scatter | solution.py:386
  1333.8 63.9 %reduce-scatter.41.cloned.1.call-done = bf16[128,384]{1,0:T(8,128)(2,1)} async-done(((bf16[1024,384]{1,0:T(8,128)(2,1)}), bf16[128,384]{1,0:T(8,128)(2,1)}) %reduce-scatter.41.cloned.1.call-update) | async-done | bytes 98320
  1399.4 30.9 %all-reduce.18.cloned.1.call-done = bf16[128,4,128]{2,0,1:T(8,128)(2,1)} async-done(((bf16[128,4,128]{2,0,1:T(8,128)(2,1)}), bf16[128,4,128]{2,0,1:T(8,128)(2,1)}) %all-reduce.18.cloned.1.call-update) | async-done | bytes 131088 | tf_op jit(solution)/shard_map/psum | solution.py:436
  1432.0 66.6 %reduce-scatter.31.cloned.1.call-done = bf16[128,2,384]{2,0,1:T(8,128)(2,1)} async-done(((bf16[1024,2,384]{2,0,1:T(8,128)(2,1)}), bf16[128,2,384]{2,0,1:T(8,128)(2,1)}) %reduce-scatter.31.cloned.1.call-update) | async-done | bytes 196624 | tf_op jit(solution)/shard_map/reduce_scatter | solution.py:389
  1500.4 44.1 %reduce-scatter.27.cloned.1.call-done = bf16[512,1024]{1,0:T(8,128)(2,1)} async-done(((bf16[2048,1024]{1,0:T(8,128)(2,1)}), bf16[512,1024]{1,0:T(8,128)(2,1)}) %reduce-scatter.27.cloned.1.call-update) | async-done | bytes 1048592 | tf_op jit(solution)/shard_map/reduce_scatter | solution.py:380
  1546.7 37.6 %all-reduce.14 = (bf16[1024]{0:T(1024)(128)(2,1)S(1)}, f32[4,384]{1,0:T(4,128)}, bf16[4,2,128]{2,1,0:T(2,128)(2,1)S(1)}, f32[6]{0:T(128)}, f32[6]{0:T(128)}, /*index=5*/f32[6]{0:T(128)}, bf16[1024]{0:T(1024)(128)(2,1)S(1)}) all-reduce(f32[1024]{0:T(1024)S(1)} %get-tuple-element.531, ...), channel_id=1, replica_groups=mesh['wide'=8,'tp'=4] {'wide'}, use_global_device_ids=true, to_apply=%region_30.31 | all-reduce | flops 4626 | bytes 30864 | tf_op jit(solution)/shard_map/psum | solution.py:414
  1584.3 6.3 all-reduce.15
  (742 shorter events, 465.4 us)
Async XLA Ops:
  7.3 97.0 %copy-start.141 = (f32[6]{0:T(128)S(1)}, f32[6]{0:T(128)}, u32[]{:S(2)}) copy-start(f32[6]{0:T(128)} %param.34) | copy-start | bytes 76
  7.3 97.0 %copy-start.88 = (bf16[384,128]{1,0:T(8,128)(2,1)S(1)}, bf16[384,128]{1,0:T(8,128)(2,1)}, u32[]{:S(2)}) copy-start(bf16[384,128]{1,0:T(8,128)(2,1)} %param.37) | copy-start | bytes 294916
  7.3 129.6 %all-gather.11.cloned.1.call-start = ((), (), s32[]{:S(2)}) async-start(), calls=%async_computation.13 | async-start | bytes 1179648 | tf_op jit(solution)/shard_map/all_gather | solution.py:214
  9.1 129.1 %all-gather.9.cloned.1.call-start = ((), (), s32[]{:S(2)}) async-start(), calls=%async_computation.12 | async-start | bytes 5242880 | tf_op jit(solution)/shard_map/all_gather | solution.py:223
  10.7 131.0 %copy-start.118 = (f32[512]{0:T(512)}, f32[512]{0:T(512)S(1)}, u32[]{:S(2)}) copy-start(f32[512]{0:T(512)S(1)} %fusion.137) | copy-start | bytes 6148
  10.7 127.5 %copy-start.132 = (f32[6]{0:T(128)S(1)}, f32[6]{0:T(128)}, u32[]{:S(2)}) copy-start(f32[6]{0:T(128)} %param.33) | copy-start | bytes 76
  10.7 131.0 %copy-start.114 = (f32[512]{0:T(512)}, f32[512]{0:T(512)S(1)}, u32[]{:S(2)}) copy-start(f32[512]{0:T(512)S(1)} %fusion.217) | copy-start | bytes 6148
  13.3 131.0 %all-gather.13.cloned.1.call-start = ((), (), s32[]{:S(2)}) async-start(), calls=%async_computation.14 | async-start | bytes 1769472 | tf_op jit(solution)/shard_map/all_gather | solution.py:212
  14.1 392.5 %reduce-scatter.21.cloned.1.call-start = ((), (), s32[]{:S(2)}) async-start(), calls=%async_computation.15 | async-start | bytes 5242880 | tf_op jit(solution)/shard_map/reduce_scatter | solution.py:261
  14.3 338.2 %copy-start.116 = (f32[384]{0:T(512)}, f32[384]{0:T(512)S(1)}, u32[]{:S(2)}) copy-start(f32[384]{0:T(512)S(1)} %mul.668) | copy-start | bytes 4612
  42.1 99.6 %copy-start.86 = (bf16[1024,6]{0,1:T(8,128)(2,1)}, bf16[1024,6]{0,1:T(8,128)(2,1)S(1)}, u32[]{:S(2)}) copy-start(bf16[1024,6]{0,1:T(8,128)(2,1)S(1)} %all_gather.41) | copy-start | bytes 36868
  43.3 114.5 %copy-start.103 = (f32[640]{0:T(1024)}, f32[640]{0:T(1024)S(1)}, u32[]{:S(2)}) copy-start(f32[640]{0:T(1024)S(1)} %get-tuple-element.533) | copy-start | bytes 7684
  43.3 114.5 %copy-start.105 = (f32[640]{0:T(1024)}, f32[640]{0:T(1024)S(1)}, u32[]{:S(2)}) copy-start(f32[640]{0:T(1024)S(1)} %get-tuple-element.534) | copy-start | bytes 7684
  43.3 114.5 %copy-start.107 = (f32[640]{0:T(1024)}, f32[640]{0:T(1024)S(1)}, u32[]{:S(2)}) copy-start(f32[640]{0:T(1024)S(1)} %get-tuple-element.535) | copy-start | bytes 7684
  43.4 114.5 %copy-start.109 = (f32[640]{0:T(1024)}, f32[640]{0:T(1024)S(1)}, u32[]{:S(2)}) copy-start(f32[640]{0:T(1024)S(1)} %get-tuple-element.536) | copy-start | bytes 7684
  361.9 96.9 %all-gather.17.cloned.1.call-start = ((), (), s32[]{:S(2)}) async-start(), calls=%async_computation.17 | async-start | bytes 2359296 | tf_op jit(solution)/shard_map/all_gather | solution.py:217
  363.5 129.7 %all-gather.15.cloned.1.call-start = ((), (), s32[]{:S(2)}) async-start(), calls=%async_computation.16 | async-start | bytes 5242880 | tf_op jit(solution)/shard_map/all_gather | solution.py:267
  408.3 228.2 %copy-start.98 = (f32[512]{0:T(512)}, f32[512]{0:T(512)S(1)}, u32[]{:S(2)}) copy-start(f32[512]{0:T(512)S(1)} %fusion.218) | copy-start | bytes 6148
  410.9 124.2 %all-gather.19.cloned.1.call-start = ((), (), s32[]{:S(2)}) async-start(), calls=%async_computation.18 | async-start | bytes 1179648 | tf_op jit(solution)/shard_map/all_gather | solution.py:218
  411.6 158.5 %all-gather.21.cloned.1.call-start = ((), (), s32[]{:S(2)}) async-start(), calls=%async_computation.20 | async-start | bytes 5242880 | tf_op jit(solution)/shard_map/all_gather | solution.py:282
  412.4 221.3 %reduce-scatter.25.cloned.1.call-start = ((), (), s32[]{:S(2)}) async-start(), calls=%async_computation.21 | async-start | bytes 5242880 | tf_op jit(solution)/shard_map/reduce_scatter | solution.py:294
  589.0 85.7 %all-gather.23.cloned.1.call-start = ((), (), s32[]{:S(2)}) async-start(), calls=%async_computation.22 | async-start | bytes 5242880 | tf_op jit(solution)/shard_map/all_gather | solution.py:300
  640.0 365.5 %reduce-scatter.33.cloned.1.call-start = ((), (), s32[]{:S(2)}) async-start(), calls=%async_computation.26 | async-start | bytes 1179648 | tf_op jit(solution)/shard_map/reduce_scatter | solution.py:395
  940.7 131.0 %reduce-scatter.43.cloned.1.call-start = ((), (), s32[]{:S(2)}) async-start(), calls=%async_computation.32 | async-start | bytes 1179648
  949.2 192.7 %reduce-scatter.35.cloned.1.call-start = ((), (), s32[]{:S(2)}) async-start(), calls=%async_computation.28 | async-start | bytes 2359296 | tf_op jit(solution)/shard_map/reduce_scatter | solution.py:404
  958.7 246.8 %reduce-scatter.37.cloned.1.call-start = ((), (), s32[]{:S(2)}) async-start(), calls=%async_computation.29 | async-start | bytes 294912
  980.1 288.8 %reduce-scatter.39.cloned.1.call-start = ((), (), s32[]{:S(2)}) async-start(), calls=%async_computation.30 | async-start | bytes 294912
  984.0 348.4 %reduce-scatter.29.cloned.1.call-start = ((), (), s32[]{:S(2)}) async-start(), calls=%async_computation.24 | async-start | bytes 294912 | tf_op jit(solution)/shard_map/reduce_scatter | solution.py:386
  988.8 408.8 %reduce-scatter.41.cloned.1.call-start = ((), (), s32[]{:S(2)}) async-start(), calls=%async_computation.31 | async-start | bytes 884736
  994.1 436.2 %all-reduce.18.cloned.1.call-start = ((), (), s32[]{:S(2)}) async-start(), calls=%async_computation.27 | async-start | bytes 262144 | tf_op jit(solution)/shard_map/psum | solution.py:436
  1005.6 493.0 %reduce-scatter.31.cloned.1.call-start = ((), (), s32[]{:S(2)}) async-start(), calls=%async_computation.25 | async-start | bytes 1769472 | tf_op jit(solution)/shard_map/reduce_scatter | solution.py:389
  1013.2 531.4 %reduce-scatter.27.cloned.1.call-start = ((), (), s32[]{:S(2)}) async-start(), calls=%async_computation.23 | async-start | bytes 5242880 | tf_op jit(solution)/shard_map/reduce_scatter | solution.py:380
  1041.4 551.1 %reduce-scatter.23.cloned.1.call-start = ((), (), s32[]{:S(2)}) async-start(), calls=%async_computation.19 | async-start | bytes 5242880 | tf_op jit(solution)/shard_map/reduce_scatter | solution.py:278
  1047.6 96.4 %copy-start.129 = (f32[640]{0:T(1024)S(1)}, f32[640]{0:T(1024)}, u32[]{:S(2)}) copy-start(f32[640]{0:T(1024)} %get-tuple-element.521) | copy-start | bytes 7684
  1047.6 96.4 %copy-start.128 = (f32[640]{0:T(1024)S(1)}, f32[640]{0:T(1024)}, u32[]{:S(2)}) copy-start(f32[640]{0:T(1024)} %get-tuple-element.522) | copy-start | bytes 7684
  1047.6 96.4 %copy-start.127 = (f32[640]{0:T(1024)S(1)}, f32[640]{0:T(1024)}, u32[]{:S(2)}) copy-start(f32[640]{0:T(1024)} %get-tuple-element.523) | copy-start | bytes 7684
  1047.6 96.4 %copy-start.126 = (f32[640]{0:T(1024)S(1)}, f32[640]{0:T(1024)}, u32[]{:S(2)}) copy-start(f32[640]{0:T(1024)} %get-tuple-element.528) | copy-start | bytes 7684
  1047.6 96.6 %copy-start.142 = (f32[6]{0:T(128)S(1)}, f32[6]{0:T(128)}, u32[]{:S(2)}) copy-start(f32[6]{0:T(128)} %param.34) | copy-start | bytes 76
  1047.7 496.9 %copy-start.3 = (bf16[512,1024]{1,0:T(8,128)(2,1)S(1)}, bf16[512,1024]{1,0:T(8,128)(2,1)}, u32[]{:S(2)}) copy-start(bf16[512,1024]{1,0:T(8,128)(2,1)} %param.25) | copy-start | bytes 3145732
  1047.7 496.9 %copy-start.100 = (f32[1024]{0:T(1024)S(1)}, f32[1024]{0:T(1024)}, u32[]{:S(2)}) copy-start(f32[1024]{0:T(1024)} %param.26) | copy-start | bytes 12292
  1047.7 496.9 %copy-start.115 = (f32[512]{0:T(512)S(1)}, f32[512]{0:T(512)}, u32[]{:S(2)}) copy-start(f32[512]{0:T(512)} %copy-done.114) | copy-start | bytes 6148
  1047.7 499.0 %copy-start.122 = (f32[1024]{0:T(1024)S(1)}, f32[1024]{0:T(1024)}, u32[]{:S(2)}) copy-start(f32[1024]{0:T(1024)} %get-tuple-element.529) | copy-start | bytes 12292
  1047.7 544.8 %copy-start.119 = (f32[512]{0:T(512)S(1)}, f32[512]{0:T(512)}, u32[]{:S(2)}) copy-start(f32[512]{0:T(512)} %copy-done.118) | copy-start | bytes 6148
  1047.7 544.8 %copy-start.19 = (bf16[512,1024]{1,0:T(8,128)(2,1)S(1)}, bf16[512,1024]{1,0:T(8,128)(2,1)}, u32[]{:S(2)}) copy-start(bf16[512,1024]{1,0:T(8,128)(2,1)} %reduce-scatter.21.cloned.1.call-done) | copy-start | bytes 3145732
  1047.7 544.8 %copy-start.39 = (bf16[512,1024]{1,0:T(8,128)(2,1)S(1)}, bf16[512,1024]{1,0:T(8,128)(2,1)}, u32[]{:S(2)}) copy-start(bf16[512,1024]{1,0:T(8,128)(2,1)} %param.41) | copy-start | bytes 3145732
  1047.7 544.8 %copy-start.90 = (f32[1024]{0:T(1024)S(1)}, f32[1024]{0:T(1024)}, u32[]{:S(2)}) copy-start(f32[1024]{0:T(1024)} %param.38) | copy-start | bytes 12292
  1047.7 544.8 %copy-start.99 = (f32[512]{0:T(512)S(1)}, f32[512]{0:T(512)}, u32[]{:S(2)}) copy-start(f32[512]{0:T(512)} %copy-done.98) | copy-start | bytes 6148
  1047.8 544.8 %copy-start.121 = (f32[512]{0:T(512)S(1)}, f32[512]{0:T(512)}, u32[]{:S(2)}) copy-start(f32[512]{0:T(512)} %copy-done.120) | copy-start | bytes 6148
  (150 other events, 1412.3 us)
Sparse Core Ops, SparseCore 0:
  10.7 43.0 all-gather.10
  55.9 33.1 all-gather.8
  91.9 50.0 all-gather.12
  362.0 44.5 reduce-scatter.20
  409.4 49.2 all-gather.16
  460.3 32.9 all-gather.14
  495.5 39.5 all-gather.18
  536.7 33.3 all-gather.20
  589.1 44.5 reduce-scatter.24
  640.2 34.4 all-gather.22
  940.9 64.6 reduce-scatter.32
  1009.2 62.5 reduce-scatter.42
  1075.3 66.5 reduce-scatter.34
  1145.1 60.3 reduce-scatter.36
  1208.6 60.2 reduce-scatter.38
  1272.1 60.2 reduce-scatter.28
  1336.1 61.5 reduce-scatter.40
  1399.9 30.3 all-reduce.17
  1433.7 64.7 reduce-scatter.30
  1501.1 43.3 reduce-scatter.26
  1547.1 44.6 reduce-scatter.22
where the time goes:
time: 1620 us; the launch traced here: 1600 us
  waiting for transfers between devices  740 us (46%)
  matrix products  297 us (18%)
  other arithmetic  198 us (12%)
  local copies, waits for them, and re-layouts  167 us (10%)
  blocking collectives  165 us (10%)
  loops' own time  17.8 us (1%)
  between operations  16.5 us (1%)
    unnamed x25, waiting for transfers between devices  213 us
    reduce_scatter x1, waiting for transfers between devices, local(): lax.psum_scatter(gate_up_term.astype(jnp.bfloat16), 'wide', scatter_dimen...  68.4 us
    reduce_scatter x1, waiting for transfers between devices, local(): lax.psum_scatter(zx_term.astype(jnp.bfloat16), 'wide', scatter_dimension=...  66.6 us
    reduce_scatter x1, waiting for transfers between devices, local(): lax.psum_scatter(query_term.astype(jnp.bfloat16), 'wide', scatter_dimensi...  61.9 us
    unnamed x305, local copies, waits for them, and re-layouts  46.2 us
    all_gather x1, waiting for transfers between devices, local(): lax.all_gather(gate_up, 'wide', axis=0, tiled=True)  46.1 us
    reduce_scatter x1, waiting for transfers between devices, local(): lax.psum_scatter(feed_row_grad.astype(jnp.bfloat16), 'tp', scatter_dimens...  44.7 us
    reduce_scatter x1, waiting for transfers between devices, local(): lax.psum_scatter(row_grad.astype(jnp.bfloat16), 'tp', scatter_dimension=0...  44.1 us
  transfers between devices with their start and end apart: 21, of which 17 were waited for; matrix products, arithmetic and copies ran while one was open for 10% of the time, Pallas kernels for 0%

commit v1 on v0

v1 whole, which is shorter than its diff:
```python
import jax
import jax.numpy as jnp
from jax import lax
from jax.experimental import pallas as pl
from jax.experimental.pallas import tpu as pltpu
from jax.sharding import PartitionSpec as P

HEADS = 8
KV_HEADS = 2
HEAD_DIM = 64
SEQ_LEN = 2048
SPAN = 128
STATE = 128
QBLOCK = 512
HALO = 8


epsilon = 1e-06
HIGHEST_PRECISION = lax.Precision.HIGHEST
NEG = -1e30


def rms_norm(values, gain):
    factor = lax.rsqrt(jnp.mean(values * values, axis=-1, keepdims=True) + epsilon)
    return values * factor * gain


def mm(left, right, left_dim, right_dim):
    return lax.dot_general(
        left, right, (((left_dim,), (right_dim,)), ((), ())), preferred_element_type=jnp.float32
    )


def low(values):
    return values.astype(jnp.bfloat16)


def whole(ref_count):
    return [pl.BlockSpec(memory_space=pltpu.VMEM)] * ref_count


def diagonal_mask():
    row = lax.broadcasted_iota(jnp.int32, (QBLOCK, QBLOCK), 0)
    col = lax.broadcasted_iota(jnp.int32, (QBLOCK, QBLOCK), 1)
    return row >= col


def block_rows(index):
    return pl.ds(pl.multiple_of(index * QBLOCK, QBLOCK), QBLOCK)


def attend_forward_kernel(heads, q_ref, kv_ref, out_ref, lse_ref):
    scale = HEAD_DIM ** (-0.5)

    def query_step(qi, unused):
        rows = block_rows(qi)
        for h in range(heads):
            cols = slice(h * HEAD_DIM, (h + 1) * HEAD_DIM)
            query = q_ref[rows, cols] * scale

            def visit(ki, carry, masked):
                top, total, acc = carry
                krows = block_rows(ki)
                scores = mm(query, kv_ref[krows, :HEAD_DIM], 1, 1)
                if masked:
                    scores = jnp.where(diagonal_mask(), scores, NEG)
                new_top = jnp.maximum(top, jnp.max(scores, axis=1, keepdims=True))
                soft = jnp.exp(scores - new_top)
                shrink = jnp.exp(top - new_top)
                total = total * shrink + jnp.sum(soft, axis=1, keepdims=True)
                acc = acc * shrink + mm(low(soft), kv_ref[krows, HEAD_DIM:], 1, 0)
                return new_top, total, acc

            carry = (
                jnp.full((QBLOCK, 1), NEG, jnp.float32),
                jnp.zeros((QBLOCK, 1), jnp.float32),
                jnp.zeros((QBLOCK, HEAD_DIM), jnp.float32),
            )
            carry = lax.fori_loop(0, qi, lambda ki, c: visit(ki, c, False), carry)
            top, total, acc = visit(qi, carry, True)
            out_ref[rows, cols] = low(acc / total)
            lse_ref[rows, h : h + 1] = top + jnp.log(total)
        return unused

    lax.fori_loop(0, q_ref.shape[0] // QBLOCK, query_step, 0)


def attend_forward(query, keyval):
    heads = query.shape[1] // HEAD_DIM
    return pl.pallas_call(
        lambda *refs: attend_forward_kernel(heads, *refs),
        out_shape=(
            jax.ShapeDtypeStruct(query.shape, jnp.bfloat16),
            jax.ShapeDtypeStruct((query.shape[0], heads), jnp.float32),
        ),
        in_specs=whole(2),
        out_specs=tuple(whole(2)),
        compiler_params=pltpu.CompilerParams(vmem_limit_bytes=40 << 20),
        cost_estimate=pl.CostEstimate(
            flops=heads * SEQ_LEN * SEQ_LEN * HEAD_DIM * 4,
            bytes_accessed=4 << 20,
            transcendentals=heads * SEQ_LEN * SEQ_LEN,
        ),
    )(query, keyval)


def attend_backward_kernel(heads, q_ref, kv_ref, out_ref, lse_ref, do_ref, dq_ref, dkv_ref, acc_ref):
    scale = HEAD_DIM ** (-0.5)
    acc_ref[...] = jnp.zeros_like(acc_ref)

    def query_step(qi, unused):
        rows = block_rows(qi)
        for h in range(heads):
            cols = slice(h * HEAD_DIM, (h + 1) * HEAD_DIM)
            query = q_ref[rows, cols] * scale
            grad = do_ref[rows, cols]
            lse = lse_ref[rows, h : h + 1]
            delta = jnp.sum(
                grad.astype(jnp.float32) * out_ref[rows, cols].astype(jnp.float32),
                axis=1,
                keepdims=True,
            )

            def visit(ki, acc, masked):
                krows = block_rows(ki)
                key = kv_ref[krows, :HEAD_DIM]
                scores = mm(query, key, 1, 1)
                if masked:
                    scores = jnp.where(diagonal_mask(), scores, NEG)
                soft = jnp.exp(scores - lse)
                soft_grad = mm(grad, kv_ref[krows, HEAD_DIM:], 1, 1)
                score_grad = low(soft * (soft_grad - delta))
                acc_ref[krows, :HEAD_DIM] += mm(score_grad, query, 0, 0)
                acc_ref[krows, HEAD_DIM:] += mm(low(soft), grad, 0, 0)
                return acc + mm(score_grad, key, 1, 0)

            acc = jnp.zeros((QBLOCK, HEAD_DIM), jnp.float32)
            acc = lax.fori_loop(0, qi, lambda ki, a: visit(ki, a, False), acc)
            dq_ref[rows, cols] = low(visit(qi, acc, True) * scale)
        return unused

    lax.fori_loop(0, q_ref.shape[0] // QBLOCK, query_step, 0)
    dkv_ref[...] = low(acc_ref[...])


def attend_backward(query, keyval, out, lse, grad):
    heads = query.shape[1] // HEAD_DIM
    return pl.pallas_call(
        lambda *refs: attend_backward_kernel(heads, *refs),
        out_shape=(
            jax.ShapeDtypeStruct(query.shape, jnp.bfloat16),
            jax.ShapeDtypeStruct(keyval.shape, jnp.bfloat16),
        ),
        in_specs=whole(5),
        out_specs=tuple(whole(2)),
        scratch_shapes=[pltpu.VMEM(keyval.shape, jnp.float32)],
        compiler_params=pltpu.CompilerParams(vmem_limit_bytes=40 << 20),
        cost_estimate=pl.CostEstimate(
            flops=heads * SEQ_LEN * SEQ_LEN * HEAD_DIM * 10,
            bytes_accessed=6 << 20,
            transcendentals=heads * SEQ_LEN * SEQ_LEN,
        ),
    )(query, keyval, out, lse, grad)


def span_mask():
    row = lax.broadcasted_iota(jnp.int32, (SPAN, SPAN), 0)
    col = lax.broadcasted_iota(jnp.int32, (SPAN, SPAN), 1)
    return row >= col


def conv_of(extended, taps):
    result = extended[HALO - 3 : HALO - 3 + SPAN, :] * taps[0:1, :]
    for k in range(1, 4):
        result = result + extended[HALO - 3 + k : HALO - 3 + k + SPAN, :] * taps[k : k + 1, :]
    return result


def mamba_forward_kernel(
    nh, z_ref, u_ref, cols_ref, rows_ref, taps_ref, skip_ref, gated_ref, y_ref, prior_ref,
    state_ref, halo_ref,
):
    channels = nh * HEAD_DIM

    @pl.when(pl.program_id(0) == 0)
    def _():
        state_ref[...] = jnp.zeros_like(state_ref)
        halo_ref[...] = jnp.zeros_like(halo_ref)

    raw = u_ref[...]
    pre = conv_of(jnp.concatenate([halo_ref[...], raw], axis=0), taps_ref[...])
    halo_ref[...] = raw[SPAN - HALO :, :]
    conv = pre * jax.nn.sigmoid(pre)
    keys = low(conv[:, channels : channels + STATE])
    queries = low(conv[:, channels + STATE :])
    affinity = mm(queries, keys, 1, 1)
    causal = span_mask()
    prior_ref[0] = state_ref[...]
    for h in range(nh):
        part = slice(h * HEAD_DIM, (h + 1) * HEAD_DIM)
        inner = conv[:, part]
        cum = cols_ref[0, :, h : h + 1]
        step = cols_ref[0, :, nh + h : nh + h + 1]
        cum_row = rows_ref[0, h : h + 1, :]
        step_row = rows_ref[0, nh + h : nh + h + 1, :]
        total = cum[SPAN - 1 : SPAN, :]
        within = jnp.exp(jnp.where(causal, cum - cum_row, NEG))
        mixing = affinity * within * step_row
        state = state_ref[part, :]
        y = mm(low(mixing), low(inner), 1, 0)
        y = y + jnp.exp(cum) * mm(queries, low(state), 1, 1)
        y = y + skip_ref[:, part] * inner
        weight = jnp.exp(total - cum) * step
        state_ref[part, :] = jnp.exp(total) * state + mm(low(inner * weight), keys, 0, 0)
        z = z_ref[:, part]
        y_ref[:, part] = y
        gated_ref[:, part] = low(y * (z * jax.nn.sigmoid(z)))


def mamba_forward(z, u, cols, rows, taps, skip):
    tokens, channels = z.shape
    width = u.shape[1]
    nh = channels // HEAD_DIM
    spans = tokens // SPAN
    return pl.pallas_call(
        lambda *refs: mamba_forward_kernel(nh, *refs),
        grid=(spans,),
        in_specs=[
            pl.BlockSpec((SPAN, channels), lambda c: (c, 0)),
            pl.BlockSpec((SPAN, width), lambda c: (c, 0)),
            pl.BlockSpec((1, SPAN, 2 * nh), lambda c: (c, 0, 0)),
            pl.BlockSpec((1, 2 * nh, SPAN), lambda c: (c, 0, 0)),
            pl.BlockSpec((4, width), lambda c: (0, 0)),
            pl.BlockSpec((1, channels), lambda c: (0, 0)),
        ],
        out_specs=(
            pl.BlockSpec((SPAN, channels), lambda c: (c, 0)),
            pl.BlockSpec((SPAN, channels), lambda c: (c, 0)),
            pl.BlockSpec((1, channels, STATE), lambda c: (c, 0, 0)),
        ),
        out_shape=(
            jax.ShapeDtypeStruct((tokens, channels), jnp.bfloat16),
            jax.ShapeDtypeStruct((tokens, channels), jnp.float32),
            jax.ShapeDtypeStruct((spans, channels, STATE), jnp.float32),
        ),
        scratch_shapes=[
            pltpu.VMEM((channels, STATE), jnp.float32),
            pltpu.VMEM((HALO, width), jnp.float32),
        ],
        compiler_params=pltpu.CompilerParams(vmem_limit_bytes=32 << 20),
        cost_estimate=pl.CostEstimate(
            flops=tokens * channels * 1000, bytes_accessed=tokens * channels * 24, transcendentals=0
        ),
    )(z, u, cols, rows, taps, skip)


def mamba_backward_kernel(
    nh, z_ref, u_ref, before_ref, cols_ref, rows_ref, taps_ref, skip_ref, y_ref, prior_ref, dg_ref,
    dz_ref, du_ref, dcols_ref, drows_ref, dtaps_ref, dskip_ref, dstate_ref, halo_ref, dconv_ref,
):
    channels = nh * HEAD_DIM
    step_id = pl.program_id(0)

    @pl.when(step_id == 0)
    def _():
        dstate_ref[...] = jnp.zeros_like(dstate_ref)
        halo_ref[...] = jnp.zeros_like(halo_ref)
        dtaps_ref[...] = jnp.zeros_like(dtaps_ref)
        dskip_ref[...] = jnp.zeros_like(dskip_ref)

    first = step_id == pl.num_programs(0) - 1
    before = jnp.where(first, 0.0, before_ref[...])
    extended = jnp.concatenate([before, u_ref[...]], axis=0)
    taps = taps_ref[...]
    pre = conv_of(extended, taps)
    gate = jax.nn.sigmoid(pre)
    conv = pre * gate
    keys = low(conv[:, channels : channels + STATE])
    queries = low(conv[:, channels + STATE :])
    affinity = mm(queries, keys, 1, 1)
    causal = span_mask()
    last = lax.broadcasted_iota(jnp.int32, (SPAN, 1), 0) == SPAN - 1
    d_affinity = jnp.zeros((SPAN, SPAN), jnp.float32)
    d_keys = jnp.zeros((SPAN, STATE), jnp.float32)
    d_queries = jnp.zeros((SPAN, STATE), jnp.float32)
    for h in range(nh):
        part = slice(h * HEAD_DIM, (h + 1) * HEAD_DIM)
        inner = conv[:, part]
        inner_low = low(inner)
        cum = cols_ref[0, :, h : h + 1]
        step = cols_ref[0, :, nh + h : nh + h + 1]
        cum_row = rows_ref[0, h : h + 1, :]
        step_row = rows_ref[0, nh + h : nh + h + 1, :]
        total = cum[SPAN - 1 : SPAN, :]
        within = jnp.exp(jnp.where(causal, cum - cum_row, NEG))
        state = prior_ref[0, part, :]
        state_low = low(state)
        d_state = dstate_ref[part, :]
        d_state_low = low(d_state)
        z = z_ref[:, part]
        sig = jax.nn.sigmoid(z)
        silu = z * sig
        d_gated = dg_ref[:, part].astype(jnp.float32)
        dz_ref[:, part] = low(d_gated * y_ref[:, part] * (sig * (1.0 + z * (1.0 - sig))))
        dy = d_gated * silu
        dy_low = low(dy)
        dskip_ref[:, part] += jnp.sum(dy * inner, axis=0, keepdims=True)
        mixing_grad = mm(dy_low, inner_low, 1, 1)
        weighted = within * step_row
        d_affinity = d_affinity + mixing_grad * weighted
        shaped = mixing_grad * affinity * within
        spread_grad = shaped * step_row
        d_inner = mm(low(affinity * weighted), dy_low, 0, 0) + skip_ref[:, part] * dy
        growth = jnp.exp(cum)
        carried = dy * growth
        carried_low = low(carried)
        d_cum = jnp.sum(spread_grad, axis=1, keepdims=True) + jnp.sum(
            carried * mm(queries, state_low, 1, 1), axis=1, keepdims=True
        )
        d_queries = d_queries + mm(carried_low, state_low, 1, 0)
        fall = jnp.exp(total - cum)
        weight = fall * step
        fresh_grad = mm(keys, d_state_low, 1, 1)
        d_inner = d_inner + weight * fresh_grad
        d_keys = d_keys + mm(low(inner * weight), d_state_low, 1, 0)
        d_weight = jnp.sum(inner * fresh_grad, axis=1, keepdims=True)
        moved = d_weight * weight
        kept = jnp.exp(total)
        d_total = jnp.sum(moved, axis=0, keepdims=True) + kept * jnp.sum(
            jnp.sum(state * d_state, axis=1, keepdims=True), axis=0, keepdims=True
        )
        dstate_ref[part, :] = kept * d_state + mm(carried_low, queries, 0, 0)
        dcols_ref[0, :, h : h + 1] = d_cum - moved + jnp.where(last, d_total, 0.0)
        dcols_ref[0, :, nh + h : nh + h + 1] = d_weight * fall
        drows_ref[0, h : h + 1, :] = -jnp.sum(spread_grad, axis=0, keepdims=True)
        drows_ref[0, nh + h : nh + h + 1, :] = jnp.sum(shaped, axis=0, keepdims=True)
        dconv_ref[:, part] = d_inner
    d_affinity_low = low(d_affinity)
    dconv_ref[:, channels : channels + STATE] = d_keys + mm(d_affinity_low, queries, 0, 0)
    dconv_ref[:, channels + STATE :] = d_queries + mm(d_affinity_low, keys, 1, 0)
    d_pre = dconv_ref[...] * (gate * (1.0 + pre * (1.0 - gate)))
    after = jnp.concatenate([d_pre, halo_ref[...]], axis=0)
    halo_ref[...] = d_pre[:HALO, :]
    d_raw = after[3 : 3 + SPAN, :] * taps[0:1, :]
    for k in range(1, 4):
        d_raw = d_raw + after[3 - k : 3 - k + SPAN, :] * taps[k : k + 1, :]
    du_ref[...] = low(d_raw)
    for k in range(4):
        shifted = extended[HALO - 3 + k : HALO - 3 + k + SPAN, :]
        dtaps_ref[k : k + 1, :] += jnp.sum(d_pre * shifted, axis=0, keepdims=True)


def mamba_backward(z, u, cols, rows, taps, skip, y, prior, d_gated):
    tokens, channels = z.shape
    width = u.shape[1]
    nh = channels // HEAD_DIM
    spans = tokens // SPAN
    per = SPAN // HALO
    back = lambda i: spans - 1 - i
    token_spec = lambda cols_count: pl.BlockSpec((SPAN, cols_count), lambda i: (back(i), 0))
    cols_spec = pl.BlockSpec((1, SPAN, 2 * nh), lambda i: (back(i), 0, 0))
    rows_spec = pl.BlockSpec((1, 2 * nh, SPAN), lambda i: (back(i), 0, 0))
    taps_spec = pl.BlockSpec((4, width), lambda i: (0, 0))
    skip_spec = pl.BlockSpec((1, channels), lambda i: (0, 0))
    return pl.pallas_call(
        lambda *refs: mamba_backward_kernel(nh, *refs),
        grid=(spans,),
        in_specs=[
            token_spec(channels),
            token_spec(width),
            pl.BlockSpec((HALO, width), lambda i: (jnp.maximum(back(i) * per - 1, 0), 0)),
            cols_spec,
            rows_spec,
            taps_spec,
            skip_spec,
            token_spec(channels),
            pl.BlockSpec((1, channels, STATE), lambda i: (back(i), 0, 0)),
            token_spec(channels),
        ],
        out_specs=(
            token_spec(channels), token_spec(width), cols_spec, rows_spec, taps_spec, skip_spec,
        ),
        out_shape=(
            jax.ShapeDtypeStruct((tokens, channels), jnp.bfloat16),
            jax.ShapeDtypeStruct((tokens, width), jnp.bfloat16),
            jax.ShapeDtypeStruct(cols.shape, jnp.float32),
            jax.ShapeDtypeStruct(rows.shape, jnp.float32),
            jax.ShapeDtypeStruct((4, width), jnp.float32),
            jax.ShapeDtypeStruct((1, channels), jnp.float32),
        ),
        scratch_shapes=[
            pltpu.VMEM((channels, STATE), jnp.float32),
            pltpu.VMEM((HALO, width), jnp.float32),
            pltpu.VMEM((SPAN, width), jnp.float32),
        ],
        compiler_params=pltpu.CompilerParams(vmem_limit_bytes=32 << 20),
        cost_estimate=pl.CostEstimate(
            flops=tokens * channels * 3000, bytes_accessed=tokens * channels * 32, transcendentals=0
        ),
    )(z, u, u, cols, rows, taps, skip, y, prior, d_gated)


def step_tables(step_raw, step_bias, decay_log):
    nh = step_raw.shape[1]
    steps = jax.nn.softplus(step_raw + step_bias).reshape(-1, SPAN, nh)
    position = jnp.arange(SPAN)
    lower = (position[:, None] >= position[None, :]).astype(jnp.float32)
    change = steps * -jnp.exp(decay_log)
    cumulative = jnp.einsum("qr,crh->cqh", lower, change, precision=HIGHEST_PRECISION)
    cols = jnp.concatenate([cumulative, steps], axis=2)
    return cols, jnp.swapaxes(cols, 1, 2)


def local(
    block_input,
    mix_gain,
    query_weight,
    zx_weight,
    step_weight,
    shared_weight,
    conv_inner,
    conv_shared,
    step_bias,
    decay_log,
    skip_gain,
    attention_out,
    mamba_out,
    feed_gain,
    gate_up,
    down_weight,
    output_grad,
):
    rows_here = query_weight.shape[0]
    q_cols = query_weight.shape[1]
    channels = zx_weight.shape[2]
    nh = step_weight.shape[1]
    units = gate_up.shape[2]
    local_heads = q_cols // HEAD_DIM
    group_size = HEADS // KV_HEADS
    kv_owner = lax.axis_index("tp") * local_heads // group_size
    inputs = block_input.astype(jnp.float32)
    normed, norm_pull = jax.vjp(rms_norm, inputs, mix_gain)
    mix_weights = jnp.concatenate(
        [
            query_weight,
            zx_weight.reshape(rows_here, 2 * channels),
            shared_weight.reshape(rows_here, 4 * STATE),
            step_weight,
        ],
        axis=1,
    )
    mix_all = lax.all_gather(mix_weights, "wide", axis=0, tiled=True)
    token_rows = lax.all_gather(low(normed), "tp", axis=0, tiled=True)
    feed_weights = jnp.concatenate(
        [
            attention_out.T,
            mamba_out.T,
            gate_up.reshape(rows_here, 2 * units),
            down_weight.T,
        ],
        axis=1,
    )
    feed_weights, cotangent, token_rows, mix_all = lax.optimization_barrier(
        (feed_weights, output_grad, token_rows, mix_all)
    )
    feed_all = lax.all_gather(feed_weights, "wide", axis=0, tiled=True)
    grad_rows = lax.all_gather(cotangent, "tp", axis=0, tiled=True)
    zx_at = q_cols
    shared_at = zx_at + 2 * channels
    step_at = shared_at + 4 * STATE
    kv_all = mix_all[:, shared_at : shared_at + 2 * STATE].reshape(-1, 2, STATE)
    kv_use = lax.dynamic_slice_in_dim(kv_all, kv_owner * HEAD_DIM, HEAD_DIM, 2).reshape(
        -1, 2 * HEAD_DIM
    )
    attn_weight = jnp.concatenate([mix_all[:, :q_cols], kv_use], axis=1)
    scan_weight = jnp.concatenate(
        [mix_all[:, zx_at:shared_at], mix_all[:, shared_at + 2 * STATE :]], axis=1
    )
    attn_in = low(mm(token_rows, attn_weight, 1, 0))
    query, keyval = attn_in[:, :q_cols], attn_in[:, q_cols:]
    z = mm(token_rows, scan_weight[:, :channels], 1, 0)
    u = mm(token_rows, scan_weight[:, channels : 2 * channels + 2 * STATE], 1, 0)
    step_raw = mm(token_rows, scan_weight[:, 2 * channels + 2 * STATE :], 1, 0)
    (cols, rows), tables_pull = jax.vjp(step_tables, step_raw, step_bias, decay_log)
    taps = jnp.concatenate([conv_inner, conv_shared.reshape(-1, 2 * STATE)], axis=1)
    skip = jnp.repeat(skip_gain, HEAD_DIM)[None, :]
    attn, lse = attend_forward(query, keyval)
    gated, y, prior = mamba_forward(z, u, cols, rows, taps, skip)
    mixer_out = jnp.concatenate([attn, gated], axis=1)
    feed_all, mixer_out, grad_rows = lax.optimization_barrier((feed_all, mixer_out, grad_rows))
    out_width = q_cols + channels
    out_weight = feed_all[:, :out_width]
    gate_up_use = feed_all[:, out_width : out_width + 2 * units]
    down_use = feed_all[:, out_width + 2 * units :]
    mixed = lax.psum_scatter(
        low(mm(mixer_out, out_weight, 1, 1)), "tp", scatter_dimension=0, tiled=True
    ).astype(jnp.float32)
    hidden_grad = mm(grad_rows, down_use, 1, 0)
    hidden_state = inputs + mixed
    normed_two, norm_two_pull = jax.vjp(rms_norm, hidden_state, feed_gain)
    feed_rows = lax.all_gather(low(normed_two), "tp", axis=0, tiled=True)
    gate_vals = mm(feed_rows, gate_up_use, 1, 0)
    gate_part = gate_vals[:, :units]
    up_part = gate_vals[:, units:]
    sigmoid_gate = jax.nn.sigmoid(gate_part)
    silu_gate = gate_part * sigmoid_gate
    hidden_low = low(silu_gate * up_part)
    gate_grad = hidden_grad * up_part * (sigmoid_gate * (1.0 + gate_part * (1.0 - sigmoid_gate)))
    gate_up_low = jnp.concatenate([low(gate_grad), low(hidden_grad * silu_gate)], axis=1)
    normed_two_grad = lax.psum_scatter(
        low(mm(gate_up_low, gate_up_use, 1, 1)), "tp", scatter_dimension=0, tiled=True
    ).astype(jnp.float32)
    feed_part = low(mm(hidden_low, down_use, 1, 1))
    down_term = low(mm(grad_rows, hidden_low, 0, 0))
    gate_up_term = low(mm(feed_rows, gate_up_low, 0, 0))
    state_from_norm, feed_gain_term = norm_two_pull(normed_two_grad)
    state_grad = output_grad.astype(jnp.float32) + state_from_norm
    mixed_rows = lax.all_gather(low(state_grad), "tp", axis=0, tiled=True)
    mixer_grad = low(mm(mixed_rows, out_weight, 1, 0))
    out_term = low(mm(mixed_rows, mixer_out, 0, 0))
    mixer_grad, feed_part, out_term, gate_up_term, down_term = lax.optimization_barrier(
        (mixer_grad, feed_part, out_term, gate_up_term, down_term)
    )
    feed_sum = lax.psum_scatter(
        jnp.concatenate([out_term, gate_up_term, down_term], axis=1),
        "wide",
        scatter_dimension=0,
        tiled=True,
    )
    feed_out = lax.psum_scatter(feed_part, "tp", scatter_dimension=0, tiled=True)
    query_grad, keyval_grad = attend_backward(query, keyval, attn, lse, mixer_grad[:, :q_cols])
    z_grad, u_grad, cols_grad, rows_grad, taps_term, skip_row = mamba_backward(
        z, u, cols, rows, taps, skip, y, prior, mixer_grad[:, q_cols:]
    )
    step_in_grad, step_bias_term, decay_log_term = tables_pull((cols_grad, rows_grad))
    all_grad = jnp.concatenate(
        [query_grad, keyval_grad, z_grad, u_grad, low(step_in_grad)], axis=1
    )
    all_weight = jnp.concatenate([attn_weight, scan_weight], axis=1)
    all_grad, feed_sum, feed_out = lax.optimization_barrier((all_grad, feed_sum, feed_out))
    row_grad = low(mm(all_grad, all_weight, 1, 1))
    normed_grad = lax.psum_scatter(row_grad, "tp", scatter_dimension=0, tiled=True)
    term = low(mm(token_rows, all_grad, 0, 0))
    kv_end = q_cols + 2 * HEAD_DIM
    keyval_placed = lax.dynamic_update_slice_in_dim(
        jnp.zeros((term.shape[0], 2, STATE), jnp.bfloat16),
        term[:, q_cols:kv_end].reshape(-1, 2, HEAD_DIM),
        kv_owner * HEAD_DIM,
        2,
    ).reshape(-1, 2 * STATE)
    mix_term = jnp.concatenate(
        [
            term[:, :q_cols],
            term[:, kv_end : kv_end + 2 * channels],
            keyval_placed,
            term[:, kv_end + 2 * channels :],
        ],
        axis=1,
    )
    mix_sum = lax.psum_scatter(mix_term, "wide", scatter_dimension=0, tiled=True)
    block_output = low(hidden_state + feed_out.astype(jnp.float32))
    input_from_norm, mix_gain_term = norm_pull(normed_grad.astype(jnp.float32))
    input_grad = low(state_grad + input_from_norm)
    skip_term = jnp.sum(skip_row.reshape(nh, HEAD_DIM), axis=1)
    own = jnp.concatenate(
        [taps_term[:, :channels].reshape(-1), step_bias_term, decay_log_term, skip_term]
    )
    common = jnp.concatenate(
        [mix_gain_term, feed_gain_term, taps_term[:, channels:].reshape(-1)]
    )
    small = lax.psum(jnp.concatenate([common, own]), "wide")
    common_count = common.shape[0]
    width = mix_gain.shape[0]
    shared_part = mix_sum[:, shared_at:step_at]
    tp_sum = lax.psum(
        jnp.concatenate([shared_part.reshape(-1), low(small[:common_count])]), "tp"
    ).astype(jnp.float32)
    shared_sum = tp_sum[: shared_part.size].reshape(rows_here, 4, STATE)
    common_sum = tp_sum[shared_part.size :]
    own_sum = small[common_count:]
    taps_count = conv_inner.size
    mix_sum = mix_sum.astype(jnp.float32)
    feed_sum = feed_sum.astype(jnp.float32)
    return (
        block_output,
        input_grad,
        common_sum[:width],
        mix_sum[:, :q_cols],
        mix_sum[:, zx_at:shared_at].reshape(rows_here, 2, channels),
        mix_sum[:, step_at:],
        shared_sum,
        own_sum[:taps_count].reshape(conv_inner.shape),
        common_sum[2 * width :].reshape(conv_shared.shape),
        own_sum[taps_count : taps_count + nh],
        own_sum[taps_count + nh : taps_count + 2 * nh],
        own_sum[taps_count + 2 * nh :],
        feed_sum[:, :q_cols].T,
        feed_sum[:, q_cols:out_width].T,
        common_sum[width : 2 * width],
        feed_sum[:, out_width : out_width + 2 * units].reshape(rows_here, 2, units),
        feed_sum[:, out_width + 2 * units :].T,
    )


def solution(mesh):
    placed = (
        P(("wide", "tp"), None),
        P(),
        P("wide", "tp"),
        P("wide", None, "tp"),
        P("wide", "tp"),
        P("wide", None, None),
        P(None, "tp"),
        P(),
        P("tp"),
        P("tp"),
        P("tp"),
        P("tp", "wide"),
        P("tp", "wide"),
        P(),
        P("wide", None, "tp"),
        P("tp", "wide"),
        P(("wide", "tp"), None),
    )
    return jax.shard_map(
        local,
        mesh=mesh,
        in_specs=placed,
        out_specs=(
            P(("wide", "tp"), None),
            P(("wide", "tp"), None),
            P(),
            P("wide", "tp"),
            P("wide", None, "tp"),
            P("wide", "tp"),
            P("wide", None, None),
            P(None, "tp"),
            P(),
            P("tp"),
            P("tp"),
            P("tp"),
            P("tp", "wide"),
            P("tp", "wide"),
            P(),
            P("wide", None, "tp"),
            P("tp", "wide"),
        ),
        check_vma=False,
    )
```

time: 1620 us -> 788 us (0.49)
  waiting for transfers between devices: 740 us -> 391 us
  matrix products: 297 us -> 91.1 us
  other arithmetic: 198 us -> 32.3 us
  Pallas kernels: 0 us -> 154 us
  blocking collectives: 165 us -> 37.1 us
  local copies, waits for them, and re-layouts: 167 us -> 58.9 us
  loops' own time: 17.8 us -> 0 us
    reduce_scatter x8 -> x5, waiting for transfers between devices: 330 us -> 125 us  [the longest x1 44.6 us: local(): lax.psum_scatter(low(mm(gate_up_low, gate_up_use, 1, 1)), 'tp', scatter_d...]
    dot_general x64 -> x17, matrix products: 289 us -> 91.1 us  [the longest x15 90.8 us: mm(): lax.dot_general(left, right, (((left_dim,), (right_dim,)), ((), ())), pre...]
    unnamed x25 -> x14, waiting for transfers between devices: 213 us -> 56.1 us
    pallas_call x0 -> x4, Pallas kernels: none -> 154 us  [the longest x1 90.2 us: mamba_backward(): pl.pallas_call(lambda *refs: mamba_backward_kernel(nh, *refs), grid=(span...]
    all_gather x4 -> x0, blocking collectives: 121 us -> none  [the longest x1 33 us: local(): lax.all_gather(query_weight, 'wide', axis=0, tiled=True)]
    reduce_sum x25 -> x3, other arithmetic: 46.2 us -> 1.61 us  [the longest x1 0.8 us: step_tables(): steps = jax.nn.softplus(step_raw + step_bias).reshape(-1, SPAN, nh)]
    add x24 -> x0, other arithmetic: 33.8 us -> none  [the longest x16 28.6 us: advance(): return (carried * factor[:, :, None, None] + fresh, carried)]
    another operation x10 -> x0, other arithmetic: 33.5 us -> none
  transfers between devices with their start and end apart: 21 -> 13, of which waited for: 17 -> 10; matrix products, arithmetic and copies ran while one was open for 10% -> 12% of each run, Pallas kernels for 0% -> 20%
where the time goes in v1:
time: 788 us; the launch traced here: 781 us
  waiting for transfers between devices  391 us (50%)
  Pallas kernels  154 us (20%)
  matrix products  91.1 us (12%)
  local copies, waits for them, and re-layouts  58.9 us (7%)
  blocking collectives  37.1 us (5%)
  other arithmetic  32.3 us (4%)
  between operations  15.2 us (2%)
    dot_general x15, matrix products, mm(): lax.dot_general(left, right, (((left_dim,), (right_dim,)), ((), ())), pre...  90.8 us
    pallas_call x1, Pallas kernels, mamba_backward(): pl.pallas_call(lambda *refs: mamba_backward_kernel(nh, *refs), grid=(span...  90.2 us
    all_gather x1, waiting for transfers between devices, local(): mix_all = lax.all_gather(mix_weights, 'wide', axis=0, tiled=True)  58.1 us
    unnamed x14, waiting for transfers between devices  56.1 us
    all_gather x1, waiting for transfers between devices, local(): feed_all = lax.all_gather(feed_weights, 'wide', axis=0, tiled=True)  47.8 us
    reduce_scatter x1, waiting for transfers between devices, local(): lax.psum_scatter(low(mm(gate_up_low, gate_up_use, 1, 1)), 'tp', scatter_d...  44.6 us
    reduce_scatter x1, waiting for transfers between devices, local(): lax.psum_scatter(low(mm(mixer_out, out_weight, 1, 1)), 'tp', scatter_dime...  42.9 us
    reduce_scatter x1, waiting for transfers between devices, local(): lax.psum_scatter(row_grad, 'tp', scatter_dimension=0, tiled=True)  37.8 us
  transfers between devices with their start and end apart: 13, of which 10 were waited for; matrix products, arithmetic and copies ran while one was open for 12% of the time, Pallas kernels for 20%

profile of v1, /device:TPU:0, one launch (start us, length us, event | category | flops | bytes accessed | tf_op | source)
XLA Modules:
  0.0 780.5 jit_solution(5986649487998066011)
XLA Ops:
  12.0 1.5 fusion.20
  13.5 2.0 fusion.13
  16.9 58.1 %all-gather.9.cloned.1.call-done = bf16[1024,1414]{0,1:T(8,128)(2,1)} async-done(((bf16[128,1414]{0,1:T(8,128)(2,1)}), bf16[1024,1414]{0,1:T(8,128)(2,1)}) %all-gather.9.cloned.1.call-update) | async-done | bytes 2895888 | tf_op jit(solution)/shard_map/all_gather | solution.py:452
  75.0 34.8 %all-gather.7.cloned.1.call-done = bf16[2048,1024]{1,0:T(8,128)(2,1)} async-done(((bf16[512,1024]{1,0:T(8,128)(2,1)}), bf16[2048,1024]{1,0:T(8,128)(2,1)}) %all-gather.7.cloned.1.call-update) | async-done | bytes 4194320 | tf_op jit(solution)/shard_map/all_gather | solution.py:453
  110.7 1.8 slice.149
  117.6 5.4 fusion.33.refs_0_
  123.1 3.5 fusion.26.refs_1_.refs_2_
  126.6 25.8 %shard_map.297 = (bf16[2048,384]{1,0:T(8,128)(2,1)S(1)}, f32[2048,384]{1,0:T(8,128)S(1)}, f32[16,384,128]{2,1,0:T(8,128)S(1)}) custom-call(f32[2048,384]{1,0:T(8,128)S(1)} %fusion.33.refs_0_, f32[2048,640]{1,0:T(8,128)S(1)} %fusion.26.refs_1_.refs_2_, f32[16,128,12]{2,1,0:T(8,128)S(1)} %copy-done.2, f32[16,12,128]{2,1,0:T(8,128)S(1)} %get-tuple-element.157.refs_3_.refs_4_, ...), custom_call_target="tpu_custom_call" | custom-call | flops 786432000 | bytes 18874368 | tf_op jit(solution)/shard_map/pallas_call | solution.py:225
  155.3 15.0 %shard_map.296 = (bf16[2048,128]{1,0:T(8,128)(2,1)S(1)}, f32[2048,2]{1,0:T(8,128)S(1)}) custom-call(bf16[2048,128]{1,0:T(8,128)(2,1)S(1)} %get-tuple-element.153.refs_0_, bf16[2048,128]{1,0:T(8,128)(2,1)S(1)} %get-tuple-element.152.refs_1_), custom_call_target="tpu_custom_call" | custom-call | flops 2147483648 | bytes 4194304 | tf_op jit(solution)/shard_map/pallas_call | solution.py:90
  173.6 47.8 %all-gather.11.cloned.1.call-done = bf16[1024,2048]{1,0:T(8,128)(2,1)} async-done(((bf16[128,2048]{1,0:T(8,128)(2,1)}), bf16[1024,2048]{1,0:T(8,128)(2,1)}) %all-gather.11.cloned.1.call-update) | async-done | bytes 4194320 | tf_op jit(solution)/shard_map/all_gather | solution.py:466
  221.3 6.3 convolution_convert_fusion.3
  227.7 42.9 %reduce-scatter.9.cloned.1.call-done = bf16[512,1024]{1,0:T(8,128)(2,1)} async-done(((bf16[2048,1024]{1,0:T(8,128)(2,1)}), bf16[512,1024]{1,0:T(8,128)(2,1)}) %reduce-scatter.9.cloned.1.call-update) | async-done | bytes 1048592 | tf_op jit(solution)/shard_map/reduce_scatter | solution.py:495
  270.6 2.0 multiply_reduce_fusion
  272.6 2.9 multiply_convert_fusion.3
  275.5 34.6 %all-gather.15.cloned.1.call-done = bf16[2048,1024]{1,0:T(8,128)(2,1)} async-done(((bf16[512,1024]{1,0:T(8,128)(2,1)}), bf16[2048,1024]{1,0:T(8,128)(2,1)}) %all-gather.15.cloned.1.call-update) | async-done | bytes 4194320 | tf_op jit(solution)/shard_map/all_gather | solution.py:501
  310.1 7.7 fusion.24
  317.9 5.8 multiply_convert_fusion.2
  325.0 7.9 %convolution_convert_fusion.4 = bf16[2048,1024]{1,0:T(8,128)(2,1)} fusion(bf16[2048,512]{0,1:T(8,128)(2,1)} %get-tuple-element.146, bf16[2048,512]{0,1:T(8,128)(2,1)S(1)} %get-tuple-element.145, bf16[1024,2048]{1,0:T(8,128)(2,1)S(1)} %copy-done.62), kind=kOutput, calls=%fused_computation.16 | convolution fusion | flops 4305453056 | bytes 10485760 | tf_op jit(solution)/shard_map/dot_general | solution.py:29
  332.9 44.6 %reduce-scatter.11.cloned.1.call-done = bf16[512,1024]{1,0:T(8,128)(2,1)} async-done(((bf16[2048,1024]{1,0:T(8,128)(2,1)}), bf16[512,1024]{1,0:T(8,128)(2,1)}) %reduce-scatter.11.cloned.1.call-update) | async-done | bytes 1048592 | tf_op jit(solution)/shard_map/reduce_scatter | solution.py:510
  377.6 3.5 fusion.15
  381.1 3.1 fusion.59
  384.5 6.3 convolution_convert_fusion.2
  390.8 7.3 convolution_convert_fusion.7
  398.1 7.1 fusion.22
  405.2 13.6 %all-gather.17.cloned.1.call-done = bf16[2048,1024]{1,0:T(8,128)(2,1)} async-done(((bf16[512,1024]{1,0:T(8,128)(2,1)}), bf16[2048,1024]{1,0:T(8,128)(2,1)}) %all-gather.17.cloned.1.call-update) | async-done | bytes 4194320 | tf_op jit(solution)/shard_map/all_gather | solution.py:518
  418.9 5.4 convolution_convert_fusion.8
  424.3 5.0 convolution_convert_fusion.5
  429.3 2.2 pad_maximum_fusion.1
  433.9 1.7 slice.164.refs_9_
  435.6 1.9 slice.163.refs_4_
  437.5 2.9 copy-done.1
  440.4 1.9 copy-done.7
  442.3 90.2 %shard_map.299 = (bf16[2048,384]{1,0:T(8,128)(2,1)S(1)}, bf16[2048,640]{1,0:T(8,128)(2,1)S(1)}, f32[16,128,12]{2,1,0:T(8,128)S(1)}, f32[16,12,128]{2,1,0:T(8,128...) custom-call(f32[2048,384]{1,0:T(8,128)S(1)} %fusion.33.refs_0_, f32[2048,640]{1,0:T(8,128)S(1)} %copy-done.1, ...), custom_call_target="tpu_custom_call" | custom-call | flops 2359296000 | bytes 25165824 | tf_op jit(solution)/shard_map/pallas_call | solution.py:365
  532.4 1.5 copy-done.8
  536.1 1.7 copy.113
  539.6 23.2 %shard_map.298 = (bf16[2048,128]{1,0:T(8,128)(2,1)S(1)}, bf16[2048,128]{1,0:T(8,128)(2,1)S(1)}) custom-call(bf16[2048,128]{1,0:T(8,128)(2,1)S(1)} %copy-done.17, bf16[2048,128]{1,0:T(8,128)(2,1)S(1)} %copy-done.15, bf16[2048,128]{1,0:T(8,128)(2,1)S(1)} %copy-done.19, f32[2048,2]{1,0:T(8,128)S(1)} %copy-done.21, bf16[2048,128]{1,0:T(8,128)(2,1)S(1)} %copy-done.13), custom_call_target="tpu_custom_call" | custom-call | flops 5368709120 | bytes 6291456 | tf_op jit(solution)/shard_map/pallas_call | solution.py:148
  566.0 1.8 constant_dynamic-update-slice_fusion.2
  569.5 9.5 %convolution_convert_fusion = bf16[1024,1286]{0,1:T(8,128)(2,1)S(1)} fusion(bf16[2048,1024]{1,0:T(8,128)(2,1)} %all-gather.7.cloned.1.call-done, bf16[2048,1286]{1,0:T(8,128)(2,1)} %convert_dynamic-update-slice_fusion), kind=kOutput, calls=%fused_computation.12 | convolution fusion | flops 5395191808 | bytes 12095488 | tf_op jit(solution)/shard_map/dot_general | solution.py:29
  579.8 2.9 copy.125
  584.4 11.0 %convolution_convert_fusion.1 = bf16[2048,1024]{1,0:T(8,128)(2,1)} fusion(bf16[2048,1286]{1,0:T(8,128)(2,1)} %convert_dynamic-update-slice_fusion, bf16[1024,262]{0,1:T(8,128)(2,1)S(1)} %copy-done.42, bf16[1024,768]{0,1:T(8,128)(2,1)S(1)} %copy-done.39, bf16[1024,128]{0,1:T(8,128)(2,1)S(1)} %bitcast.86, bf16[1024,128]{0,1:T(8,128)(2,1)S(1)} %copy-done.47), kind=kOutput, calls=%fused_computation.13 | convolution fusion | flops 5406507008 | bytes 12095488 | tf_op jit(solution)/shard_map/dot_general | solution.py:29
  602.6 54.9 %reduce-scatter.19.cloned.1.call-done = bf16[128,1414]{1,0:T(8,128)(2,1)} async-done(((bf16[1024,1414]{1,0:T(8,128)(2,1)}), bf16[128,1414]{1,0:T(8,128)(2,1)}) %reduce-scatter.19.cloned.1.call-update) | async-done | bytes 362000
  657.4 1.7 slice.202
  665.6 37.8 %reduce-scatter.17.cloned.1.call-done = bf16[512,1024]{1,0:T(8,128)(2,1)} async-done(((bf16[2048,1024]{1,0:T(8,128)(2,1)}), bf16[512,1024]{1,0:T(8,128)(2,1)}) %reduce-scatter.17.cloned.1.call-update) | async-done | bytes 1048592 | tf_op jit(solution)/shard_map/reduce_scatter | solution.py:542
  703.5 2.2 fusion.16
  706.4 37.1 %psum.14 = f32[4626]{0:T(1024)S(1)} all-reduce(f32[4626]{0:T(1024)S(1)} %concatenate.55), channel_id=1, replica_groups=mesh['wide'=8,'tp'=4] {'wide'}, use_global_device_ids=true, to_apply=%region_15.16 | all-reduce | flops 4626 | bytes 37008 | tf_op jit(solution)/shard_map/psum | solution.py:571
  744.9 4.1 fusion.19
  750.2 20.5 %all-reduce.2.cloned.1.call-done = bf16[68608]{0:T(1024)(128)(2,1)} async-done(((bf16[68608]{0:T(1024)(128)(2,1)}), bf16[68608]{0:T(1024)(128)(2,1)}) %all-reduce.2.cloned.1.call-update) | async-done | bytes 137232 | tf_op jit(solution)/shard_map/psum | solution.py:575
  770.7 1.6 slice.204
  (252 shorter events, 51.4 us)
Async XLA Ops:
  7.2 6.3 copy-start.22
  7.2 67.8 %all-gather.9.cloned.1.call-start = ((), (), s32[]{:S(2)}) async-start(), calls=%async_computation.7 | async-start | bytes 3262464 | tf_op jit(solution)/shard_map/all_gather | solution.py:452
  8.4 7.1 copy-start.45
  10.4 5.2 copy-start.48
  10.4 5.4 copy-start.49
  11.9 97.9 %all-gather.7.cloned.1.call-start = ((), (), s32[]{:S(2)}) async-start(), calls=%async_computation.6 | async-start | bytes 5242880 | tf_op jit(solution)/shard_map/all_gather | solution.py:453
  15.5 95.0 %copy-start.61 = (f32[6]{0:T(128)S(1)}, f32[6]{0:T(128)}, u32[]{:S(2)}) copy-start(f32[6]{0:T(128)} %param.27) | copy-start | bytes 76
  15.5 95.2 %copy-start.58 = (f32[4,384]{1,0:T(4,128)S(1)}, f32[4,384]{1,0:T(4,128)}, u32[]{:S(2)}) copy-start(f32[4,384]{1,0:T(4,128)} %param.23) | copy-start | bytes 18436
  15.5 95.2 %copy-start.66 = (f32[6]{0:T(128)S(1)}, f32[6]{0:T(128)}, u32[]{:S(2)}) copy-start(f32[6]{0:T(128)} %param.26) | copy-start | bytes 76
  15.5 95.2 %copy-start.59 = (f32[4,2,128]{2,1,0:T(2,128)S(1)}, f32[4,2,128]{2,1,0:T(2,128)}, u32[]{:S(2)}) copy-start(f32[4,2,128]{2,1,0:T(2,128)} %param.24) | copy-start | bytes 12292
  15.5 158.0 %all-gather.13.cloned.1.call-start = ((), (), s32[]{:S(2)}) async-start(), calls=%async_computation.9 | async-start | bytes 5242880 | tf_op jit(solution)/shard_map/all_gather | solution.py:467
  75.0 37.5 %copy-start.35 = (bf16[1024,1414]{0,1:T(8,128)(2,1)S(1)}, bf16[1024,1414]{0,1:T(8,128)(2,1)}, u32[]{:S(2)}) copy-start(bf16[1024,1414]{0,1:T(8,128)(2,1)} %all-gather.9.cloned.1.call-done) | copy-start | bytes 8687620
  109.8 111.5 %all-gather.11.cloned.1.call-start = ((), (), s32[]{:S(2)}) async-start(), calls=%async_computation.8 | async-start | bytes 4718592 | tf_op jit(solution)/shard_map/all_gather | solution.py:466
  110.4 160.2 %reduce-scatter.9.cloned.1.call-start = ((), (), s32[]{:S(2)}) async-start(), calls=%async_computation.10 | async-start | bytes 5242880 | tf_op jit(solution)/shard_map/reduce_scatter | solution.py:495
  110.7 4.0 copy-start.33
  110.7 4.0 copy-start.60
  117.6 5.5 copy-start.34
  117.6 5.5 copy-start.38
  117.6 5.5 copy-start.41
  126.6 25.8 %copy-start = (f32[2048,640]{1,0:T(8,128)}, f32[2048,640]{1,0:T(8,128)S(1)}, u32[]{:S(2)}) copy-start(f32[2048,640]{1,0:T(8,128)S(1)} %fusion.26.refs_1_.refs_2_) | copy-start | bytes 15728644
  126.6 25.8 %slice-start = ((bf16[1024,1414]{0,1:T(8,128)(2,1)}), bf16[1024,256]{0,1:T(8,128)(2,1)S(1)}, s32[]{:S(2)}) async-start(bf16[1024,1414]{0,1:T(8,128)(2,1)} %all-gather.9.cloned.1.call-done), calls=%async_computation.19 | async-start | bytes 1048576 | tf_op jit(solution)/shard_map/slice | solution.py:471
  126.6 25.9 %copy-start.46 = (bf16[1024,128]{0,1:T(8,128)(2,1)S(1)}, bf16[1024,128]{0,1:T(8,128)(2,1)}, u32[]{:S(2)}) copy-start(bf16[1024,128]{0,1:T(8,128)(2,1)} %slice.149) | copy-start | bytes 786436
  155.2 15.1 %copy-start.14 = (bf16[2048,128]{1,0:T(8,128)(2,1)}, bf16[2048,128]{1,0:T(8,128)(2,1)S(1)}, u32[]{:S(2)}) copy-start(bf16[2048,128]{1,0:T(8,128)(2,1)S(1)} %get-tuple-element.152.refs_1_) | copy-start | bytes 1572868
  155.3 15.1 %copy-start.16 = (bf16[2048,128]{1,0:T(8,128)(2,1)}, bf16[2048,128]{1,0:T(8,128)(2,1)S(1)}, u32[]{:S(2)}) copy-start(bf16[2048,128]{1,0:T(8,128)(2,1)S(1)} %get-tuple-element.153.refs_0_) | copy-start | bytes 1572868
  227.6 44.9 %copy-start.50 = (f32[1024]{0:T(1024)S(1)}, f32[1024]{0:T(1024)}, u32[]{:S(2)}) copy-start(f32[1024]{0:T(1024)} %param.30) | copy-start | bytes 12292
  227.7 82.5 %all-gather.15.cloned.1.call-start = ((), (), s32[]{:S(2)}) async-start(), calls=%async_computation.11 | async-start | bytes 5242880 | tf_op jit(solution)/shard_map/all_gather | solution.py:501
  275.5 102.1 %reduce-scatter.11.cloned.1.call-start = ((), (), s32[]{:S(2)}) async-start(), calls=%async_computation.12 | async-start | bytes 5242880 | tf_op jit(solution)/shard_map/reduce_scatter | solution.py:510
  310.1 7.8 copy-start.62
  310.1 7.8 copy-start.63
  332.9 86.0 %all-gather.17.cloned.1.call-start = ((), (), s32[]{:S(2)}) async-start(), calls=%async_computation.13 | async-start | bytes 5242880 | tf_op jit(solution)/shard_map/all_gather | solution.py:518
  384.2 185.3 %reduce-scatter.13.cloned.1.call-start = ((), (), s32[]{:S(2)}) async-start(), calls=%async_computation.14 | async-start | bytes 4718592 | tf_op jit(solution)/shard_map/reduce_scatter | solution.py:524
  390.8 7.3 copy-start.64
  390.8 7.3 copy-start.69
  390.8 7.3 copy-start.70
  418.9 5.4 copy-start.65
  424.2 5.1 copy-start.37
  424.3 5.1 copy-start.40
  431.6 138.0 %reduce-scatter.15.cloned.1.call-start = ((), (), s32[]{:S(2)}) async-start(), calls=%async_computation.15 | async-start | bytes 5242880 | tf_op jit(solution)/shard_map/reduce_scatter | solution.py:530
  432.1 225.3 %reduce-scatter.19.cloned.1.call-start = ((), (), s32[]{:S(2)}) async-start(), calls=%async_computation.18 | async-start | bytes 3538944
  539.6 25.1 %copy-start.11 = (bf16[2048,384]{1,0:T(8,128)(2,1)S(1)}, bf16[2048,384]{1,0:T(8,128)(2,1)}, u32[]{:S(2)}) copy-start(bf16[2048,384]{1,0:T(8,128)(2,1)} %copy-done.10) | copy-start | bytes 4718596
  582.7 120.7 %reduce-scatter.17.cloned.1.call-start = ((), (), s32[]{:S(2)}) async-start(), calls=%async_computation.16 | async-start | bytes 5242880 | tf_op jit(solution)/shard_map/reduce_scatter | solution.py:542
  595.4 175.3 %all-reduce.2.cloned.1.call-start = ((), (), s32[]{:S(2)}) async-start(), calls=%async_computation.17 | async-start | bytes 274432 | tf_op jit(solution)/shard_map/psum | solution.py:575
  599.7 103.7 %copy-start.24 = (bf16[512,1024]{1,0:T(8,128)(2,1)S(1)}, bf16[512,1024]{1,0:T(8,128)(2,1)}, u32[]{:S(2)}) copy-start(bf16[512,1024]{1,0:T(8,128)(2,1)} %param.17) | copy-start | bytes 3145732
  599.8 103.7 %copy-start.51 = (f32[1024]{0:T(1024)S(1)}, f32[1024]{0:T(1024)}, u32[]{:S(2)}) copy-start(f32[1024]{0:T(1024)} %param.18) | copy-start | bytes 12292
  599.8 103.7 %copy-start.55 = (f32[512]{0:T(512)S(1)}, f32[512]{0:T(512)}, u32[]{:S(2)}) copy-start(f32[512]{0:T(512)} %copy-done.54) | copy-start | bytes 6148
  659.1 85.8 %copy-start.26 = (bf16[512,1024]{1,0:T(8,128)(2,1)S(1)}, bf16[512,1024]{1,0:T(8,128)(2,1)}, u32[]{:S(2)}) copy-start(bf16[512,1024]{1,0:T(8,128)(2,1)} %reduce-scatter.9.cloned.1.call-done) | copy-start | bytes 3145732
  659.1 85.8 %copy-start.32 = (bf16[512,1024]{1,0:T(8,128)(2,1)S(1)}, bf16[512,1024]{1,0:T(8,128)(2,1)}, u32[]{:S(2)}) copy-start(bf16[512,1024]{1,0:T(8,128)(2,1)} %param.33) | copy-start | bytes 3145732
  661.4 44.3 %copy-start.53 = (f32[1536]{0:T(1024)S(1)}, f32[1536]{0:T(1024)}, u32[]{:S(2)}) copy-start(f32[1536]{0:T(1024)} %reshape.163) | copy-start | bytes 18436
  (37 other events, 95.4 us)
Sparse Core Ops, SparseCore 0:
  12.0 62.8 all-gather.8
  77.1 32.6 all-gather.6
  111.4 34.4 all-gather.12
  147.9 73.3 all-gather.10
  227.8 42.7 reduce-scatter.8
  275.6 34.4 all-gather.14
  333.0 44.5 reduce-scatter.10
  384.3 34.4 all-gather.16
  431.7 88.2 reduce-scatter.12
  522.5 44.2 reduce-scatter.14
  582.9 74.5 reduce-scatter.18
  659.8 43.5 reduce-scatter.16
  744.3 26.2 all-reduce.1

commit v2 on v1

--- a/solution.py
+++ b/solution.py
@@ -42,58 +42,59 @@
 def diagonal_mask():
     row = lax.broadcasted_iota(jnp.int32, (QBLOCK, QBLOCK), 0)
     col = lax.broadcasted_iota(jnp.int32, (QBLOCK, QBLOCK), 1)
-    return row >= col
+    return row <= col
 
 
 def block_rows(index):
     return pl.ds(pl.multiple_of(index * QBLOCK, QBLOCK), QBLOCK)
 
 
-def attend_forward_kernel(heads, q_ref, kv_ref, out_ref, lse_ref):
+def attend_forward_kernel(heads, q_ref, k_ref, vt_ref, out_ref, lse_ref):
     scale = HEAD_DIM ** (-0.5)
 
     def query_step(qi, unused):
-        rows = block_rows(qi)
+        cols = block_rows(qi)
         for h in range(heads):
-            cols = slice(h * HEAD_DIM, (h + 1) * HEAD_DIM)
-            query = q_ref[rows, cols] * scale
+            part = slice(h * HEAD_DIM, (h + 1) * HEAD_DIM)
+            query = q_ref[cols, part] * scale
 
             def visit(ki, carry, masked):
                 top, total, acc = carry
                 krows = block_rows(ki)
-                scores = mm(query, kv_ref[krows, :HEAD_DIM], 1, 1)
+                scores = mm(k_ref[krows, :], query, 1, 1)
                 if masked:
                     scores = jnp.where(diagonal_mask(), scores, NEG)
-                new_top = jnp.maximum(top, jnp.max(scores, axis=1, keepdims=True))
+                new_top = jnp.maximum(top, jnp.max(scores, axis=0, keepdims=True))
                 soft = jnp.exp(scores - new_top)
                 shrink = jnp.exp(top - new_top)
-                total = total * shrink + jnp.sum(soft, axis=1, keepdims=True)
-                acc = acc * shrink + mm(low(soft), kv_ref[krows, HEAD_DIM:], 1, 0)
+                total = total * shrink + jnp.sum(soft, axis=0, keepdims=True)
+                acc = acc * shrink + mm(vt_ref[:, krows], low(soft), 1, 0)
                 return new_top, total, acc
 
             carry = (
-                jnp.full((QBLOCK, 1), NEG, jnp.float32),
-                jnp.zeros((QBLOCK, 1), jnp.float32),
-                jnp.zeros((QBLOCK, HEAD_DIM), jnp.float32),
+                jnp.full((1, QBLOCK), NEG, jnp.float32),
+                jnp.zeros((1, QBLOCK), jnp.float32),
+                jnp.zeros((HEAD_DIM, QBLOCK), jnp.float32),
             )
             carry = lax.fori_loop(0, qi, lambda ki, c: visit(ki, c, False), carry)
             top, total, acc = visit(qi, carry, True)
-            out_ref[rows, cols] = low(acc / total)
-            lse_ref[rows, h : h + 1] = top + jnp.log(total)
+            out_ref[part, cols] = low(acc / total)
+            lse_ref[h : h + 1, cols] = top + jnp.log(total)
         return unused
 
     lax.fori_loop(0, q_ref.shape[0] // QBLOCK, query_step, 0)
 
 
 def attend_forward(query, keyval):
-    heads = query.shape[1] // HEAD_DIM
-    return pl.pallas_call(
+    tokens, width = query.shape
+    heads = width // HEAD_DIM
+    out, lse = pl.pallas_call(
         lambda *refs: attend_forward_kernel(heads, *refs),
         out_shape=(
-            jax.ShapeDtypeStruct(query.shape, jnp.bfloat16),
-            jax.ShapeDtypeStruct((query.shape[0], heads), jnp.float32),
-        ),
-        in_specs=whole(2),
+            jax.ShapeDtypeStruct((width, tokens), jnp.bfloat16),
+            jax.ShapeDtypeStruct((heads, tokens), jnp.float32),
+        ),
+        in_specs=whole(3),
         out_specs=tuple(whole(2)),
         compiler_params=pltpu.CompilerParams(vmem_limit_bytes=40 << 20),
         cost_estimate=pl.CostEstimate(
@@ -101,42 +102,40 @@
             bytes_accessed=4 << 20,
             transcendentals=heads * SEQ_LEN * SEQ_LEN,
         ),
-    )(query, keyval)
-
-
-def attend_backward_kernel(heads, q_ref, kv_ref, out_ref, lse_ref, do_ref, dq_ref, dkv_ref, acc_ref):
+    )(query, keyval[:, :HEAD_DIM], keyval[:, HEAD_DIM:].T)
+    return out.T, lse
+
+
+def attend_backward_kernel(
+    heads, q_ref, k_ref, kt_ref, v_ref, lse_ref, delta_ref, do_ref, dq_ref, dkv_ref, acc_ref
+):
     scale = HEAD_DIM ** (-0.5)
     acc_ref[...] = jnp.zeros_like(acc_ref)
 
     def query_step(qi, unused):
-        rows = block_rows(qi)
+        cols = block_rows(qi)
         for h in range(heads):
-            cols = slice(h * HEAD_DIM, (h + 1) * HEAD_DIM)
-            query = q_ref[rows, cols] * scale
-            grad = do_ref[rows, cols]
-            lse = lse_ref[rows, h : h + 1]
-            delta = jnp.sum(
-                grad.astype(jnp.float32) * out_ref[rows, cols].astype(jnp.float32),
-                axis=1,
-                keepdims=True,
-            )
+            part = slice(h * HEAD_DIM, (h + 1) * HEAD_DIM)
+            query = q_ref[cols, part] * scale
+            grad = do_ref[cols, part]
+            lse = lse_ref[h : h + 1, cols]
+            delta = delta_ref[h : h + 1, cols]
 
             def visit(ki, acc, masked):
                 krows = block_rows(ki)
-                key = kv_ref[krows, :HEAD_DIM]
-                scores = mm(query, key, 1, 1)
+                scores = mm(k_ref[krows, :], query, 1, 1)
                 if masked:
                     scores = jnp.where(diagonal_mask(), scores, NEG)
                 soft = jnp.exp(scores - lse)
-                soft_grad = mm(grad, kv_ref[krows, HEAD_DIM:], 1, 1)
+                soft_grad = mm(v_ref[krows, :], grad, 1, 1)
                 score_grad = low(soft * (soft_grad - delta))
-                acc_ref[krows, :HEAD_DIM] += mm(score_grad, query, 0, 0)
-                acc_ref[krows, HEAD_DIM:] += mm(low(soft), grad, 0, 0)
-                return acc + mm(score_grad, key, 1, 0)
-
-            acc = jnp.zeros((QBLOCK, HEAD_DIM), jnp.float32)
+                acc_ref[krows, :HEAD_DIM] += mm(score_grad, query, 1, 0)
+                acc_ref[krows, HEAD_DIM:] += mm(low(soft), grad, 1, 0)
+                return acc + mm(kt_ref[:, krows], score_grad, 1, 0)
+
+            acc = jnp.zeros((HEAD_DIM, QBLOCK), jnp.float32)
             acc = lax.fori_loop(0, qi, lambda ki, a: visit(ki, a, False), acc)
-            dq_ref[rows, cols] = low(visit(qi, acc, True) * scale)
+            dq_ref[part, cols] = low(visit(qi, acc, True) * scale)
         return unused
 
     lax.fori_loop(0, q_ref.shape[0] // QBLOCK, query_step, 0)
@@ -144,14 +143,18 @@
 
 
 def attend_backward(query, keyval, out, lse, grad):
-    heads = query.shape[1] // HEAD_DIM
-    return pl.pallas_call(
+    tokens, width = query.shape
+    heads = width // HEAD_DIM
+    product = grad.astype(jnp.float32) * out.astype(jnp.float32)
+    delta = jnp.sum(product.reshape(tokens, heads, HEAD_DIM), axis=2).T
+    key = keyval[:, :HEAD_DIM]
+    query_grad, keyval_grad = pl.pallas_call(
         lambda *refs: attend_backward_kernel(heads, *refs),
         out_shape=(
-            jax.ShapeDtypeStruct(query.shape, jnp.bfloat16),
+            jax.ShapeDtypeStruct((width, tokens), jnp.bfloat16),
             jax.ShapeDtypeStruct(keyval.shape, jnp.bfloat16),
         ),
-        in_specs=whole(5),
+        in_specs=whole(7),
         out_specs=tuple(whole(2)),
         scratch_shapes=[pltpu.VMEM(keyval.shape, jnp.float32)],
         compiler_params=pltpu.CompilerParams(vmem_limit_bytes=40 << 20),
@@ -160,7 +163,8 @@
             bytes_accessed=6 << 20,
             transcendentals=heads * SEQ_LEN * SEQ_LEN,
         ),
-    )(query, keyval, out, lse, grad)
+    )(query, key, key.T, keyval[:, HEAD_DIM:], lse, delta, grad)
+    return query_grad.T, keyval_grad
 
 
 def span_mask():
@@ -255,8 +259,9 @@
 
 
 def mamba_backward_kernel(
-    nh, z_ref, u_ref, before_ref, cols_ref, rows_ref, taps_ref, skip_ref, y_ref, prior_ref, dg_ref,
-    dz_ref, du_ref, dcols_ref, drows_ref, dtaps_ref, dskip_ref, dstate_ref, halo_ref, dconv_ref,
+    nh, z_ref, u_ref, before_ref, cols_ref, rows_ref, wide_ref, taps_ref, skip_ref, y_ref, prior_ref,
+    dg_ref, dz_ref, du_ref, dcols_ref, drows_ref, dwide_ref, dtaps_ref, dskip_ref, dstate_ref,
+    halo_ref, dconv_ref,
 ):
     channels = nh * HEAD_DIM
     step_id = pl.program_id(0)
@@ -281,60 +286,61 @@
     causal = span_mask()
     last = lax.broadcasted_iota(jnp.int32, (SPAN, 1), 0) == SPAN - 1
     d_affinity = jnp.zeros((SPAN, SPAN), jnp.float32)
-    d_keys = jnp.zeros((SPAN, STATE), jnp.float32)
-    d_queries = jnp.zeros((SPAN, STATE), jnp.float32)
+    inner = conv[:, :channels]
+    inner_low = low(inner)
+    state = prior_ref[0]
+    state_low = low(state)
+    d_state = dstate_ref[...]
+    d_state_low = low(d_state)
+    z = z_ref[...]
+    sig = jax.nn.sigmoid(z)
+    d_gated = dg_ref[...].astype(jnp.float32)
+    dz_ref[...] = low(d_gated * y_ref[...] * (sig * (1.0 + z * (1.0 - sig))))
+    dy = d_gated * (z * sig)
+    dy_low = low(dy)
+    dskip_ref[...] += jnp.sum(dy * inner, axis=0, keepdims=True)
+    cum_wide = wide_ref[:, :channels]
+    step_wide = wide_ref[:, channels:]
+    carried = dy * jnp.exp(cum_wide)
+    carried_low = low(carried)
+    fall_wide = jnp.exp(cum_wide[SPAN - 1 : SPAN, :] - cum_wide)
+    weight = fall_wide * step_wide
+    fresh_grad = mm(keys, d_state_low, 1, 1)
+    d_weight = inner * fresh_grad
+    moved = d_weight * weight
+    dwide_ref[:, :channels] = (
+        carried * mm(queries, state_low, 1, 1)
+        - moved
+        + jnp.where(last, jnp.sum(moved, axis=0, keepdims=True), 0.0)
+    )
+    dwide_ref[:, channels:] = d_weight * fall_wide
+    d_queries = mm(carried_low, state_low, 1, 0)
+    d_keys = mm(low(inner * weight), d_state_low, 1, 0)
+    d_state_in = mm(carried_low, queries, 0, 0)
+    dconv_ref[:, :channels] = weight * fresh_grad + skip_ref[...] * dy
     for h in range(nh):
         part = slice(h * HEAD_DIM, (h + 1) * HEAD_DIM)
-        inner = conv[:, part]
-        inner_low = low(inner)
         cum = cols_ref[0, :, h : h + 1]
-        step = cols_ref[0, :, nh + h : nh + h + 1]
         cum_row = rows_ref[0, h : h + 1, :]
         step_row = rows_ref[0, nh + h : nh + h + 1, :]
-        total = cum[SPAN - 1 : SPAN, :]
         within = jnp.exp(jnp.where(causal, cum - cum_row, NEG))
-        state = prior_ref[0, part, :]
-        state_low = low(state)
-        d_state = dstate_ref[part, :]
-        d_state_low = low(d_state)
-        z = z_ref[:, part]
-        sig = jax.nn.sigmoid(z)
-        silu = z * sig
-        d_gated = dg_ref[:, part].astype(jnp.float32)
-        dz_ref[:, part] = low(d_gated * y_ref[:, part] * (sig * (1.0 + z * (1.0 - sig))))
-        dy = d_gated * silu
-        dy_low = low(dy)
-        dskip_ref[:, part] += jnp.sum(dy * inner, axis=0, keepdims=True)
-        mixing_grad = mm(dy_low, inner_low, 1, 1)
+        mixing_grad = mm(dy_low[:, part], inner_low[:, part], 1, 1)
         weighted = within * step_row
         d_affinity = d_affinity + mixing_grad * weighted
         shaped = mixing_grad * affinity * within
         spread_grad = shaped * step_row
-        d_inner = mm(low(affinity * weighted), dy_low, 0, 0) + skip_ref[:, part] * dy
-        growth = jnp.exp(cum)
-        carried = dy * growth
-        carried_low = low(carried)
-        d_cum = jnp.sum(spread_grad, axis=1, keepdims=True) + jnp.sum(
-            carried * mm(queries, state_low, 1, 1), axis=1, keepdims=True
+        dconv_ref[:, part] += mm(low(affinity * weighted), dy_low[:, part], 0, 0)
+        kept = jnp.exp(cum[SPAN - 1 : SPAN, :])
+        d_total = kept * jnp.sum(
+            jnp.sum(state[part, :] * d_state[part, :], axis=0, keepdims=True), axis=1, keepdims=True
         )
-        d_queries = d_queries + mm(carried_low, state_low, 1, 0)
-        fall = jnp.exp(total - cum)
-        weight = fall * step
-        fresh_grad = mm(keys, d_state_low, 1, 1)
-        d_inner = d_inner + weight * fresh_grad
-        d_keys = d_keys + mm(low(inner * weight), d_state_low, 1, 0)
-        d_weight = jnp.sum(inner * fresh_grad, axis=1, keepdims=True)
-        moved = d_weight * weight
-        kept = jnp.exp(total)
-        d_total = jnp.sum(moved, axis=0, keepdims=True) + kept * jnp.sum(
-            jnp.sum(state * d_state, axis=1, keepdims=True), axis=0, keepdims=True
+        dstate_ref[part, :] = kept * d_state[part, :] + d_state_in[part, :]
+        dcols_ref[0, :, h : h + 1] = jnp.sum(spread_grad, axis=1, keepdims=True) + jnp.where(
+            last, d_total, 0.0
         )
-        dstate_ref[part, :] = kept * d_state + mm(carried_low, queries, 0, 0)
-        dcols_ref[0, :, h : h + 1] = d_cum - moved + jnp.where(last, d_total, 0.0)
-        dcols_ref[0, :, nh + h : nh + h + 1] = d_weight * fall
+        dcols_ref[0, :, nh + h : nh + h + 1] = jnp.zeros((SPAN, 1), jnp.float32)
         drows_ref[0, h : h + 1, :] = -jnp.sum(spread_grad, axis=0, keepdims=True)
         drows_ref[0, nh + h : nh + h + 1, :] = jnp.sum(shaped, axis=0, keepdims=True)
-        dconv_ref[:, part] = d_inner
     d_affinity_low = low(d_affinity)
     dconv_ref[:, channels : channels + STATE] = d_keys + mm(d_affinity_low, queries, 0, 0)
     dconv_ref[:, channels + STATE :] = d_queries + mm(d_affinity_low, keys, 1, 0)
@@ -350,7 +356,7 @@
         dtaps_ref[k : k + 1, :] += jnp.sum(d_pre * shifted, axis=0, keepdims=True)
 
 
-def mamba_backward(z, u, cols, rows, taps, skip, y, prior, d_gated):
+def mamba_backward(z, u, cols, rows, wide, taps, skip, y, prior, d_gated):
     tokens, channels = z.shape
     width = u.shape[1]
     nh = channels // HEAD_DIM
@@ -371,6 +377,7 @@
             pl.BlockSpec((HALO, width), lambda i: (jnp.maximum(back(i) * per - 1, 0), 0)),
             cols_spec,
             rows_spec,
+            token_spec(2 * channels),
             taps_spec,
             skip_spec,
             token_spec(channels),
@@ -378,13 +385,15 @@
             token_spec(channels),
         ],
         out_specs=(
-            token_spec(channels), token_spec(width), cols_spec, rows_spec, taps_spec, skip_spec,
+            token_spec(channels), token_spec(width), cols_spec, rows_spec,
+            token_spec(2 * channels), taps_spec, skip_spec,
         ),
         out_shape=(
             jax.ShapeDtypeStruct((tokens, channels), jnp.bfloat16),
             jax.ShapeDtypeStruct((tokens, width), jnp.bfloat16),
             jax.ShapeDtypeStruct(cols.shape, jnp.float32),
             jax.ShapeDtypeStruct(rows.shape, jnp.float32),
+            jax.ShapeDtypeStruct(wide.shape, jnp.float32),
             jax.ShapeDtypeStruct((4, width), jnp.float32),
             jax.ShapeDtypeStruct((1, channels), jnp.float32),
         ),
@@ -397,7 +406,7 @@
         cost_estimate=pl.CostEstimate(
             flops=tokens * channels * 3000, bytes_accessed=tokens * channels * 32, transcendentals=0
         ),
-    )(z, u, u, cols, rows, taps, skip, y, prior, d_gated)
+    )(z, u, u, cols, rows, wide, taps, skip, y, prior, d_gated)
 
 
 def step_tables(step_raw, step_bias, decay_log):
@@ -408,7 +417,51 @@
     change = steps * -jnp.exp(decay_log)
     cumulative = jnp.einsum("qr,crh->cqh", lower, change, precision=HIGHEST_PRECISION)
     cols = jnp.concatenate([cumulative, steps], axis=2)
-    return cols, jnp.swapaxes(cols, 1, 2)
+    wide = jnp.repeat(cols.reshape(-1, 2 * nh), HEAD_DIM, axis=1)
+    return cols, jnp.swapaxes(cols, 1, 2), wide
+
+
+def swap(values, axis, distance):
+    size = lax.axis_size(axis)
+    return lax.ppermute(values, axis, [(i, i ^ distance) for i in range(size)])
+
+
+def total_over(values, axis):
+    distance = 1
+    while distance < lax.axis_size(axis):
+        values = values + swap(values, axis, distance)
+        distance *= 2
+    return values
+
+
+def gather_tokens(values):
+    if lax.axis_size("tp") != 4:
+        return lax.all_gather(values, "tp", axis=0, tiled=True)
+    count = values.shape[0]
+    across = swap(values, "tp", 2)
+    beside = swap(values, "tp", 1)
+    corner = swap(across, "tp", 1)
+    me = lax.axis_index("tp")
+    result = jnp.zeros((4 * count, values.shape[1]), values.dtype)
+    for distance, piece in ((0, values), (1, beside), (2, across), (3, corner)):
+        place = jnp.bitwise_xor(me, distance) * count
+        result = lax.dynamic_update_slice_in_dim(result, piece, place, 0)
+    return result
+
+
+def scatter_tokens(values):
+    if lax.axis_size("tp") != 4:
+        return lax.psum_scatter(values, "tp", scatter_dimension=0, tiled=True).astype(jnp.float32)
+    count = values.shape[0] // 4
+    me = lax.axis_index("tp")
+
+    def share(distance):
+        place = jnp.bitwise_xor(me, distance) * count
+        return lax.dynamic_slice_in_dim(values, place, count, 0)
+
+    far = share(2).astype(jnp.float32) + swap(share(3), "tp", 1).astype(jnp.float32)
+    near = share(0).astype(jnp.float32) + swap(share(1), "tp", 1).astype(jnp.float32)
+    return near + swap(low(far), "tp", 2).astype(jnp.float32)
 
 
 def local(
@@ -450,7 +503,7 @@
         axis=1,
     )
     mix_all = lax.all_gather(mix_weights, "wide", axis=0, tiled=True)
-    token_rows = lax.all_gather(low(normed), "tp", axis=0, tiled=True)
+    token_rows = gather_tokens(low(normed))
     feed_weights = jnp.concatenate(
         [
             attention_out.T,
@@ -464,7 +517,7 @@
         (feed_weights, output_grad, token_rows, mix_all)
     )
     feed_all = lax.all_gather(feed_weights, "wide", axis=0, tiled=True)
-    grad_rows = lax.all_gather(cotangent, "tp", axis=0, tiled=True)
+    grad_rows = gather_tokens(cotangent)
     zx_at = q_cols
     shared_at = zx_at + 2 * channels
     step_at = shared_at + 4 * STATE
@@ -481,7 +534,7 @@
     z = mm(token_rows, scan_weight[:, :channels], 1, 0)
     u = mm(token_rows, scan_weight[:, channels : 2 * channels + 2 * STATE], 1, 0)
     step_raw = mm(token_rows, scan_weight[:, 2 * channels + 2 * STATE :], 1, 0)
-    (cols, rows), tables_pull = jax.vjp(step_tables, step_raw, step_bias, decay_log)
+    (cols, rows, wide), tables_pull = jax.vjp(step_tables, step_raw, step_bias, decay_log)
     taps = jnp.concatenate([conv_inner, conv_shared.reshape(-1, 2 * STATE)], axis=1)
     skip = jnp.repeat(skip_gain, HEAD_DIM)[None, :]
     attn, lse = attend_forward(query, keyval)
@@ -492,9 +545,7 @@
     out_weight = feed_all[:, :out_width]
     gate_up_use = feed_all[:, out_width : out_width + 2 * units]
     down_use = feed_all[:, out_width + 2 * units :]
-    mixed = lax.psum_scatter(
-        low(mm(mixer_out, out_weight, 1, 1)), "tp", scatter_dimension=0, tiled=True
-    ).astype(jnp.float32)
+    mixed = scatter_tokens(low(mm(mixer_out, out_weight, 1, 1)))
     hidden_grad = mm(grad_rows, down_use, 1, 0)
     hidden_state = inputs + mixed
     normed_two, norm_two_pull = jax.vjp(rms_norm, hidden_state, feed_gain)
@@ -507,9 +558,7 @@
     hidden_low = low(silu_gate * up_part)
     gate_grad = hidden_grad * up_part * (sigmoid_gate * (1.0 + gate_part * (1.0 - sigmoid_gate)))
     gate_up_low = jnp.concatenate([low(gate_grad), low(hidden_grad * silu_gate)], axis=1)
-    normed_two_grad = lax.psum_scatter(
-        low(mm(gate_up_low, gate_up_use, 1, 1)), "tp", scatter_dimension=0, tiled=True
-    ).astype(jnp.float32)
+    normed_two_grad = scatter_tokens(low(mm(gate_up_low, gate_up_use, 1, 1)))
     feed_part = low(mm(hidden_low, down_use, 1, 1))
     down_term = low(mm(grad_rows, hidden_low, 0, 0))
     gate_up_term = low(mm(feed_rows, gate_up_low, 0, 0))
@@ -527,19 +576,19 @@
         scatter_dimension=0,
         tiled=True,
     )
-    feed_out = lax.psum_scatter(feed_part, "tp", scatter_dimension=0, tiled=True)
+    feed_out = scatter_tokens(feed_part)
     query_grad, keyval_grad = attend_backward(query, keyval, attn, lse, mixer_grad[:, :q_cols])
-    z_grad, u_grad, cols_grad, rows_grad, taps_term, skip_row = mamba_backward(
-        z, u, cols, rows, taps, skip, y, prior, mixer_grad[:, q_cols:]
-    )
-    step_in_grad, step_bias_term, decay_log_term = tables_pull((cols_grad, rows_grad))
+    z_grad, u_grad, cols_grad, rows_grad, wide_grad, taps_term, skip_row = mamba_backward(
+        z, u, cols, rows, wide, taps, skip, y, prior, mixer_grad[:, q_cols:]
+    )
+    step_in_grad, step_bias_term, decay_log_term = tables_pull((cols_grad, rows_grad, wide_grad))
     all_grad = jnp.concatenate(
         [query_grad, keyval_grad, z_grad, u_grad, low(step_in_grad)], axis=1
     )
     all_weight = jnp.concatenate([attn_weight, scan_weight], axis=1)
     all_grad, feed_sum, feed_out = lax.optimization_barrier((all_grad, feed_sum, feed_out))
     row_grad = low(mm(all_grad, all_weight, 1, 1))
-    normed_grad = lax.psum_scatter(row_grad, "tp", scatter_dimension=0, tiled=True)
+    normed_grad = scatter_tokens(row_grad)
     term = low(mm(token_rows, all_grad, 0, 0))
     kv_end = q_cols + 2 * HEAD_DIM
     keyval_placed = lax.dynamic_update_slice_in_dim(
@@ -558,8 +607,8 @@
         axis=1,
     )
     mix_sum = lax.psum_scatter(mix_term, "wide", scatter_dimension=0, tiled=True)
-    block_output = low(hidden_state + feed_out.astype(jnp.float32))
-    input_from_norm, mix_gain_term = norm_pull(normed_grad.astype(jnp.float32))
+    block_output = low(hidden_state + feed_out)
+    input_from_norm, mix_gain_term = norm_pull(normed_grad)
     input_grad = low(state_grad + input_from_norm)
     skip_term = jnp.sum(skip_row.reshape(nh, HEAD_DIM), axis=1)
     own = jnp.concatenate(
@@ -568,15 +617,12 @@
     common = jnp.concatenate(
         [mix_gain_term, feed_gain_term, taps_term[:, channels:].reshape(-1)]
     )
-    small = lax.psum(jnp.concatenate([common, own]), "wide")
+    small = total_over(jnp.concatenate([common, own]), "wide")
     common_count = common.shape[0]
     width = mix_gain.shape[0]
     shared_part = mix_sum[:, shared_at:step_at]
-    tp_sum = lax.psum(
-        jnp.concatenate([shared_part.reshape(-1), low(small[:common_count])]), "tp"
-    ).astype(jnp.float32)
-    shared_sum = tp_sum[: shared_part.size].reshape(rows_here, 4, STATE)
-    common_sum = tp_sum[shared_part.size :]
+    shared_sum = total_over(shared_part.astype(jnp.float32), "tp").reshape(rows_here, 4, STATE)
+    common_sum = total_over(small[:common_count], "tp")
     own_sum = small[common_count:]
     taps_count = conv_inner.size
     mix_sum = mix_sum.astype(jnp.float32)

time: 788 us -> 583 us (0.74)
  waiting for transfers between devices: 391 us -> 208 us
  Pallas kernels: 154 us -> 86.6 us
  local copies, waits for them, and re-layouts: 58.9 us -> 113 us
  blocking collectives: 37.1 us -> 0 us
  other arithmetic: 32.3 us -> 54.2 us
  starting transfers between devices: 0.91 us -> 16.4 us
  matrix products: 91.1 us -> 82.4 us
    ppermute x0 -> x25, waiting for transfers between devices: none -> 131 us  [swap(): return lax.ppermute(values, axis, [(i, i ^ distance) for i in range(size)])]
    reduce_scatter x4 -> x0, waiting for transfers between devices: 125 us -> none  [the longest x1 44.6 us: local(): lax.psum_scatter(low(mm(gate_up_low, gate_up_use, 1, 1)), 'tp', scatter_d...]
    pallas_call x1, Pallas kernels: 90.2 us -> 29.4 us  [mamba_backward(): pl.pallas_call(lambda *refs: mamba_backward_kernel(nh, *refs), grid=(span...]
    unnamed x14 -> x7, waiting for transfers between devices: 56.1 us -> 8.05 us
    all_gather x1, waiting for transfers between devices: 47.8 us -> 0.01 us  [local(): feed_all = lax.all_gather(feed_weights, 'wide', axis=0, tiled=True)]
    all_gather x1, waiting for transfers between devices: 58.1 us -> 20.2 us  [local(): mix_all = lax.all_gather(mix_weights, 'wide', axis=0, tiled=True)]
    psum x1 -> x0, blocking collectives: 37.1 us -> none  [local(): small = lax.psum(jnp.concatenate([common, own]), 'wide')]
    all_gather x2 -> x0, waiting for transfers between devices: 34.8 us -> none  [the longest x1 34.8 us: local(): token_rows = lax.all_gather(low(normed), 'tp', axis=0, tiled=True)]
  transfers between devices with their start and end apart: 13 -> 31, of which waited for: 10 -> 16; matrix products, arithmetic and copies ran while one was open for 12% -> 28% of each run, Pallas kernels for 20% -> 15%
where the time goes in v2:
time: 583 us; the launch traced here: 577 us
  waiting for transfers between devices  208 us (36%)
  local copies, waits for them, and re-layouts  113 us (19%)
  Pallas kernels  86.6 us (15%)
  matrix products  82.4 us (14%)
  other arithmetic  54.2 us (9%)
  starting transfers between devices  16.4 us (3%)
  between operations  15.9 us (3%)
    ppermute x25, waiting for transfers between devices, swap(): return lax.ppermute(values, axis, [(i, i ^ distance) for i in range(size)])  131 us
    dot_general x15, matrix products, mm(): lax.dot_general(left, right, (((left_dim,), (right_dim,)), ((), ())), pre...  82 us
    unnamed x182, local copies, waits for them, and re-layouts  43.1 us
    all_gather x1, waiting for transfers between devices, local(): feed_rows = lax.all_gather(low(normed_two), 'tp', axis=0, tiled=True)  31.9 us
    pallas_call x1, Pallas kernels, mamba_backward(): pl.pallas_call(lambda *refs: mamba_backward_kernel(nh, *refs), grid=(span...  29.4 us
    pallas_call x1, Pallas kernels, mamba_forward(): pl.pallas_call(lambda *refs: mamba_forward_kernel(nh, *refs), grid=(spans...  25.5 us
    all_gather x1, waiting for transfers between devices, local(): mix_all = lax.all_gather(mix_weights, 'wide', axis=0, tiled=True)  20.2 us
    convert_element_type x8, other arithmetic, low(): return values.astype(jnp.bfloat16)  19.9 us
  transfers between devices with their start and end apart: 31, of which 16 were waited for; matrix products, arithmetic and copies ran while one was open for 28% of the time, Pallas kernels for 15%

profile of v2, /device:TPU:0, one launch (start us, length us, event | category | flops | bytes accessed | tf_op | source)
XLA Modules:
  0.0 577.2 jit_solution(2957528804408331357)
XLA Ops:
  18.1 2.9 collective-permute-start.1
  21.1 23.4 %collective-permute-done.1 = bf16[512,1024]{0,1:T(8,128)(2,1)S(1)} collective-permute-done((bf16[512,1024]{0,1:T(8,128)(2,1)}, bf16[512,1024]{0,1:T(8,128)(2,1)S(1)}, u32[]{:S(2)}, u32[]{:S(2)}) %collective-permute-start.1) | collective-permute-done | bytes 1048608 | tf_op jit(solution)/shard_map/ppermute | solution.py:426
  54.6 20.2 %all-gather.5.cloned.1.call-done = bf16[1024,1414]{0,1:T(8,128)(2,1)} async-done(((bf16[128,1414]{0,1:T(8,128)(2,1)}), bf16[1024,1414]{0,1:T(8,128)(2,1)}) %all-gather.5.cloned.1.call-update) | async-done | bytes 2895888 | tf_op jit(solution)/shard_map/all_gather | solution.py:505
  81.1 3.3 broadcast_multiply_fusion
  89.6 13.6 %shard_map.296 = (bf16[128,2048]{1,0:T(8,128)(2,1)S(1)}, f32[2,2048]{1,0:T(2,128)S(1)}) custom-call(bf16[2048,128]{1,0:T(8,128)(2,1)S(1)} %slice.179.refs_0_, bf16[2048,64]{1,0:T(8,128)(2,1)S(1)} %get-tuple-element.169.refs_1_, bf16[64,2048]{1,0:T(8,128)(2,1)S(1)} %copy.169.refs_2_), custom_call_target="tpu_custom_call" | custom-call | flops 2147483648 | bytes 4194304 | tf_op jit(solution)/shard_map/pallas_call | solution.py:91
  103.2 5.3 fusion.22.refs_1_.refs_2_
  108.5 2.4 copy.176
  111.9 5.1 fusion.29.refs_0_
  117.0 25.5 %shard_map.297 = (bf16[2048,384]{1,0:T(8,128)(2,1)S(1)}, f32[2048,384]{1,0:T(8,128)S(1)}, f32[16,384,128]{2,1,0:T(8,128)S(1)}) custom-call(f32[2048,384]{1,0:T(8,128)S(1)} %fusion.29.refs_0_, f32[2048,640]{1,0:T(8,128)S(1)} %bitcast.97, f32[16,128,12]{2,1,0:T(8,128)S(1)} %copy.175.refs_2_.refs_3_, f32[16,12,128]{2,1,0:T(8,128)S(1)} %get-tuple-element.170.refs_3_.refs_4_, ...), custom_call_target="tpu_custom_call" | custom-call | flops 786432000 | bytes 18874368 | tf_op jit(solution)/shard_map/pallas_call | solution.py:229
  159.0 4.2 convolution_convert_fusion.3
  167.7 24.4 %collective-permute-done.8 = bf16[512,1024]{0,1:T(8,128)(2,1)S(1)} collective-permute-done((bf16[512,1024]{0,1:T(8,128)(2,1)S(1)}, bf16[512,1024]{0,1:T(8,128)(2,1)S(1)}, u32[]{:S(2)}, u32[]{:S(2)}) %collective-permute-start.8) | collective-permute-done | bytes 1048608 | tf_op jit(solution)/shard_map/ppermute | solution.py:426
  194.1 2.8 multiply_convert_fusion.3
  197.0 31.9 %all-gather.9.cloned.1.call-done = bf16[2048,1024]{0,1:T(8,128)(2,1)} async-done(((bf16[512,1024]{0,1:T(8,128)(2,1)}), bf16[2048,1024]{0,1:T(8,128)(2,1)}) %all-gather.9.cloned.1.call-update) | async-done | bytes 4194320 | tf_op jit(solution)/shard_map/all_gather | solution.py:552
  228.9 7.4 %fusion.20 = f32[2048,1024]{0,1:T(8,128)S(1)} fusion(bf16[2048,1024]{0,1:T(8,128)(2,1)} %all-gather.9.cloned.1.call-done, bf16[1024,2048]{1,0:T(8,128)(2,1)} %all-gather.7.cloned.1.call-done), kind=kOutput, calls=%fused_computation.55 | convolution fusion | flops 4294967296 | bytes 14680064 | tf_op jit(solution)/shard_map/dot_general | solution.py:29
  236.3 5.3 multiply_convert_fusion.2
  241.5 4.7 convolution_convert_fusion.4
  253.6 23.8 %collective-permute-done.11 = bf16[512,1024]{0,1:T(8,128)(2,1)} collective-permute-done((bf16[512,1024]{0,1:T(8,128)(2,1)}, bf16[512,1024]{0,1:T(8,128)(2,1)}, u32[]{:S(2)}, u32[]{:S(2)}) %collective-permute-start.11) | collective-permute-done | bytes 1048608 | tf_op jit(solution)/shard_map/ppermute | solution.py:426
  277.4 4.0 multiply_reduce_fusion
  281.4 5.0 fusion.57
  286.7 6.4 %convolution_convert_fusion.1 = bf16[2048,1024]{0,1:T(8,128)(2,1)} fusion(bf16[2048,512]{0,1:T(8,128)(2,1)} %get-tuple-element.155, bf16[1024,2048]{1,0:T(8,128)(2,1)} %all-gather.7.cloned.1.call-done), kind=kOutput, calls=%fused_computation.13 | convolution fusion | flops 2149580800 | bytes 7340032 | tf_op jit(solution)/shard_map/dot_general | solution.py:29
  297.6 6.7 %fusion.18 = bf16[1024,1024]{1,0:T(8,128)(2,1)} fusion(bf16[2048,1024]{0,1:T(8,128)(2,1)S(1)} %copy-done.69, bf16[2048,512]{0,1:T(8,128)(2,1)S(1)} %copy-done.76, bf16[2048,512]{0,1:T(8,128)(2,1)S(1)} %copy-done.74), kind=kOutput, calls=%fused_computation.53 | convolution fusion | flops 4304404480 | bytes 10485760 | tf_op jit(solution)/shard_map/dot_general | solution.py:29
  304.3 16.8 %all-gather.11.cloned.1.call-done = bf16[2048,1024]{0,1:T(8,128)(2,1)} async-done(((bf16[512,1024]{0,1:T(8,128)(2,1)}), bf16[2048,1024]{0,1:T(8,128)(2,1)}) %all-gather.11.cloned.1.call-update) | async-done | bytes 4194320 | tf_op jit(solution)/shard_map/all_gather | solution.py:567
  321.1 5.3 convolution_convert_fusion.8
  326.5 5.1 convolution_convert_fusion.5
  334.2 3.5 broadcast_in_dim.12
  337.7 6.6 %copy.187.refs_5_ = f32[2048,768]{1,0:T(8,128)} copy(f32[2048,768]{0,1:T(8,128)} %bitcast.99) | data formatting | bytes 12582912 | tf_op jit(solution)/shard_map/jvp()/reshape | solution.py:420
  349.3 3.1 constant_dynamic-slice_fusion.3
  352.9 2.6 copy-done
  357.4 29.4 %shard_map.299 = (bf16[2048,384]{1,0:T(8,128)(2,1)S(1)}, bf16[2048,640]{1,0:T(8,128)(2,1)S(1)}, f32[16,128,12]{2,1,0:T(8,128)S(1)}, f32[16,12,128]{2,1,0:T(8,128...) custom-call(f32[2048,384]{1,0:T(8,128)S(1)} %copy-done.2, f32[2048,640]{1,0:T(8,128)S(1)} %copy-done, ...), custom_call_target="tpu_custom_call" | custom-call | flops 2359296000 | bytes 25165824 | tf_op jit(solution)/shard_map/pallas_call | solution.py:371
  391.2 6.6 %copy.189 = f32[2048,768]{0,1:T(8,128)} copy(f32[2048,768]{1,0:T(8,128)} %get-tuple-element.65) | data formatting | bytes 12582912 | tf_op jit(solution)/shard_map/pallas_call | solution.py:371
  397.8 3.5 reduce_sum.104
  405.8 2.5 copy.183
  409.7 18.1 %shard_map.298 = (bf16[128,2048]{1,0:T(8,128)(2,1)S(1)}, bf16[2048,128]{1,0:T(8,128)(2,1)S(1)}) custom-call(bf16[2048,128]{1,0:T(8,128)(2,1)S(1)} %slice.179.refs_0_, bf16[2048,64]{1,0:T(8,128)(2,1)S(1)} %copy-done.14, bf16[64,2048]{1,0:T(8,128)(2,1)S(1)} %copy.184.refs_2_, bf16[2048,64]{1,0:T(8,128)(2,1)S(1)} %copy-done.12, f32[2,2048]{1,0:T(2,128)S(1)} %copy-done.22, ...), custom_call_target="tpu_custom_call" | custom-call | flops 5368709120 | bytes 6291456 | tf_op jit(solution)/shard_map/pallas_call | solution.py:151
  434.4 23.2 %collective-permute-done.14 = bf16[512,1024]{0,1:T(8,128)(2,1)S(1)} collective-permute-done((bf16[512,1024]{0,1:T(8,128)(2,1)S(1)}, bf16[512,1024]{0,1:T(8,128)(2,1)S(1)}, u32[]{:S(2)}, u32[]{:S(2)}) %collective-permute-start.14) | collective-permute-done | bytes 1048608 | tf_op jit(solution)/shard_map/ppermute | solution.py:426
  457.6 3.3 convert_add_fusion.2
  460.9 9.6 %convolution_convert_fusion = bf16[1024,1286]{0,1:T(8,128)(2,1)S(1)} fusion(bf16[2048,1024]{0,1:T(8,128)(2,1)} %constant_dynamic-update-slice_fusion.10, bf16[2048,1286]{1,0:T(8,128)(2,1)} %copy-done.55), kind=kOutput, calls=%fused_computation.12 | convolution fusion | flops 5395191808 | bytes 12095488 | tf_op jit(solution)/shard_map/dot_general | solution.py:29
  471.1 3.0 copy.209
  474.1 10.0 %convolution_convert_fusion.2 = bf16[2048,1024]{0,1:T(8,128)(2,1)S(1)} fusion(bf16[2048,1286]{1,0:T(8,128)(2,1)} %copy-done.55, bf16[1024,262]{0,1:T(8,128)(2,1)S(1)} %copy-done.51, bf16[1024,768]{0,1:T(8,128)(2,1)} %slice.145, bf16[1024,128]{0,1:T(8,128)(2,1)} %bitcast.115, bf16[1024,128]{0,1:T(8,128)(2,1)} %copy-done.53), kind=kOutput, calls=%fused_computation.14 | convolution fusion | flops 5406507008 | bytes 12095488 | tf_op jit(solution)/shard_map/dot_general | solution.py:29
  486.0 3.6 collective-permute-done.16
  493.3 3.2 add_convert_fusion.1
  496.6 19.9 %collective-permute-done.17 = bf16[512,1024]{0,1:T(8,128)(2,1)} collective-permute-done((bf16[512,1024]{0,1:T(8,128)(2,1)}, bf16[512,1024]{0,1:T(8,128)(2,1)}, u32[]{:S(2)}, u32[]{:S(2)}) %collective-permute-start.17) | collective-permute-done | bytes 1048608 | tf_op jit(solution)/shard_map/ppermute | solution.py:426
  516.5 2.8 fusion.12
  527.4 2.5 copy.197
  535.5 2.6 collective-permute-start.20
  538.1 3.3 collective-permute-done.20
  541.5 8.0 %reduce-scatter.7.cloned.1.call-done = bf16[128,1414]{1,0:T(8,128)(2,1)} async-done(((bf16[1024,1414]{1,0:T(8,128)(2,1)}), bf16[128,1414]{1,0:T(8,128)(2,1)}) %reduce-scatter.7.cloned.1.call-update) | async-done | bytes 362000
  551.4 3.7 fusion.15
  565.2 3.8 collective-permute-done.24
  (339 shorter events, 127.6 us)
Async XLA Ops:
  7.2 67.6 %all-gather.5.cloned.1.call-start = ((), (), s32[]{:S(2)}) async-start(), calls=%async_computation.2 | async-start | bytes 3262464 | tf_op jit(solution)/shard_map/all_gather | solution.py:505
  11.7 147.3 %all-gather.7.cloned.1.call-start = ((), (), s32[]{:S(2)}) async-start(), calls=%async_computation.3 | async-start | bytes 4718592 | tf_op jit(solution)/shard_map/all_gather | solution.py:519
  14.2 30.2 %copy-start.59 = (f32[512]{0:T(512)}, f32[512]{0:T(512)S(1)}, u32[]{:S(2)}) copy-start(f32[512]{0:T(512)S(1)} %fusion.48) | copy-start | bytes 6148
  18.1 26.3 %collective-permute-start.1 = (bf16[512,1024]{0,1:T(8,128)(2,1)}, bf16[512,1024]{0,1:T(8,128)(2,1)S(1)}, u32[]{:S(2)}, u32[]{:S(2)}) collective-permute-start(bf16[512,1024]{0,1:T(8,128)(2,1)} %get-tuple-element.152), channel_id=1, source_target_pairs={{0,2},{1,3},{2,0},{3,1},{4,6},{5,7},{6,4},{7,5},{8,10},{9,11},{10,... | collective-permute-start | bytes 3145736 | tf_op jit(solution)/shard_map/ppermute | solution.py:426
  21.1 30.2 %collective-permute-start = (bf16[512,1024]{0,1:T(8,128)(2,1)}, bf16[512,1024]{0,1:T(8,128)(2,1)S(1)}, u32[]{:S(2)}, u32[]{:S(2)}) collective-permute-start(bf16[512,1024]{0,1:T(8,128)(2,1)} %get-tuple-element.152), channel_id=1, source_target_pairs={{0,1},{1,0},{2,3},{3,2},{4,5},{5,4},{6,7},{7,6},{8,9},{9,8},{10,11... | collective-permute-start | bytes 3145736 | tf_op jit(solution)/shard_map/ppermute | solution.py:426
  44.4 9.0 %collective-permute-start.2 = (bf16[512,1024]{0,1:T(8,128)(2,1)S(1)}, bf16[512,1024]{0,1:T(8,128)(2,1)S(1)}, u32[]{:S(2)}, u32[]{:S(2)}) collective-permute-start(bf16[512,1024]{0,1:T(8,128)(2,1)S(1)} %collective-permute-done.1), channel_id=1, source_target_pairs={{0,1},{1,0},{2,3},{3,2},{4,5},{5,4},{6,7},{7,6},{8,9},{9,8},{10,11... | collective-permute-start | bytes 3145736 | tf_op jit(solution)/shard_map/ppermute | solution.py:426
  45.4 29.5 %copy-start.67 = (f32[6]{0:T(128)S(1)}, f32[6]{0:T(128)}, u32[]{:S(2)}) copy-start(f32[6]{0:T(128)} %param.27) | copy-start | bytes 76
  51.3 29.7 %copy-start.66 = (f32[6]{0:T(128)S(1)}, f32[6]{0:T(128)}, u32[]{:S(2)}) copy-start(f32[6]{0:T(128)} %param.25) | copy-start | bytes 76
  74.8 154.0 %all-gather.9.cloned.1.call-start = ((), (), s32[]{:S(2)}) async-start(), calls=%async_computation.4 | async-start | bytes 5242880 | tf_op jit(solution)/shard_map/all_gather | solution.py:552
  77.5 72.8 %collective-permute-start.3 = (bf16[512,1024]{1,0:T(8,128)(2,1)}, bf16[512,1024]{1,0:T(8,128)(2,1)}, u32[]{:S(2)}, u32[]{:S(2)}) collective-permute-start(bf16[512,1024]{1,0:T(8,128)(2,1)} %param.33), channel_id=1, source_target_pairs={{0,1},{1,0},{2,3},{3,2},{4,5},{5,4},{6,7},{7,6},{8,9},{9,8},{10,11... | collective-permute-start | bytes 3145736 | tf_op jit(solution)/shard_map/ppermute | solution.py:426
  77.5 34.2 %collective-permute-start.4 = (bf16[512,1024]{1,0:T(8,128)(2,1)}, bf16[512,1024]{1,0:T(8,128)(2,1)}, u32[]{:S(2)}, u32[]{:S(2)}) collective-permute-start(bf16[512,1024]{1,0:T(8,128)(2,1)} %param.33), channel_id=1, source_target_pairs={{0,2},{1,3},{2,0},{3,1},{4,6},{5,7},{6,4},{7,5},{8,10},{9,11},{10,... | collective-permute-start | bytes 3145736 | tf_op jit(solution)/shard_map/ppermute | solution.py:426
  87.8 15.4 %copy-start.13 = (bf16[2048,64]{1,0:T(8,128)(2,1)}, bf16[2048,64]{1,0:T(8,128)(2,1)S(1)}, u32[]{:S(2)}) copy-start(bf16[2048,64]{1,0:T(8,128)(2,1)S(1)} %get-tuple-element.169.refs_1_) | copy-start | bytes 786436
  111.2 33.9 %copy-start.37 = (bf16[128,2048]{0,1:T(8,128)(2,1)}, bf16[128,2048]{0,1:T(8,128)(2,1)S(1)}, u32[]{:S(2)}) copy-start(bf16[128,2048]{0,1:T(8,128)(2,1)S(1)} %copy.170) | copy-start | bytes 1572868
  111.6 44.4 %collective-permute-start.5 = (bf16[512,1024]{1,0:T(8,128)(2,1)}, bf16[512,1024]{1,0:T(8,128)(2,1)}, u32[]{:S(2)}, u32[]{:S(2)}) collective-permute-start(bf16[512,1024]{1,0:T(8,128)(2,1)} %collective-permute-done.4), channel_id=1, source_target_pairs={{0,1},{1,0},{2,3},{3,2},{4,5},{5,4},{6,7},{7,6},{8,9},{9,8},{10,11... | collective-permute-start | bytes 3145736 | tf_op jit(solution)/shard_map/ppermute | solution.py:426
  117.0 25.5 %copy-start.1 = (f32[2048,384]{1,0:T(8,128)}, f32[2048,384]{1,0:T(8,128)S(1)}, u32[]{:S(2)}) copy-start(f32[2048,384]{1,0:T(8,128)S(1)} %fusion.29.refs_0_) | copy-start | bytes 9437188
  163.2 28.9 %copy-start.24 = (bf16[512,1024]{0,1:T(8,128)(2,1)S(1)}, bf16[512,1024]{0,1:T(8,128)(2,1)}, u32[]{:S(2)}) copy-start(bf16[512,1024]{0,1:T(8,128)(2,1)} %copy-done.23) | copy-start | bytes 3145732
  163.5 2.7 collective-permute-start.7
  163.9 30.1 %copy-start.56 = (f32[1024]{0:T(1024)S(1)}, f32[1024]{0:T(1024)}, u32[]{:S(2)}) copy-start(f32[1024]{0:T(1024)} %param.30) | copy-start | bytes 12292
  163.9 3.8 collective-permute-start.6
  166.6 25.5 %collective-permute-start.8 = (bf16[512,1024]{0,1:T(8,128)(2,1)S(1)}, bf16[512,1024]{0,1:T(8,128)(2,1)S(1)}, u32[]{:S(2)}, u32[]{:S(2)}) collective-permute-start(bf16[512,1024]{0,1:T(8,128)(2,1)S(1)} %add_convert_fusion.4), channel_id=1, source_target_pairs={{0,2},{1,3},{2,0},{3,1},{4,6},{5,7},{6,4},{7,5},{8,10},{9,11},{10,... | collective-permute-start | bytes 3145736 | tf_op jit(solution)/shard_map/ppermute | solution.py:426
  196.9 124.2 %all-gather.11.cloned.1.call-start = ((), (), s32[]{:S(2)}) async-start(), calls=%async_computation.5 | async-start | bytes 5242880 | tf_op jit(solution)/shard_map/all_gather | solution.py:567
  247.7 2.7 collective-permute-start.10
  247.9 5.7 collective-permute-start.9
  251.8 25.6 %collective-permute-start.11 = (bf16[512,1024]{0,1:T(8,128)(2,1)}, bf16[512,1024]{0,1:T(8,128)(2,1)}, u32[]{:S(2)}, u32[]{:S(2)}) collective-permute-start(bf16[512,1024]{0,1:T(8,128)(2,1)} %add_convert_fusion.3), channel_id=1, source_target_pairs={{0,2},{1,3},{2,0},{3,1},{4,6},{5,7},{6,4},{7,5},{8,10},{9,11},{10,... | collective-permute-start | bytes 3145736 | tf_op jit(solution)/shard_map/ppermute | solution.py:426
  286.4 174.4 %reduce-scatter.5.cloned.1.call-start = ((), (), s32[]{:S(2)}) async-start(), calls=%async_computation.6 | async-start | bytes 4718592 | tf_op jit(solution)/shard_map/reduce_scatter | solution.py:573
  333.9 215.5 %reduce-scatter.7.cloned.1.call-start = ((), (), s32[]{:S(2)}) async-start(), calls=%async_computation.7 | async-start | bytes 3538944
  352.4 77.9 %collective-permute-start.13 = (bf16[512,1024]{0,1:T(8,128)(2,1)}, bf16[512,1024]{0,1:T(8,128)(2,1)}, u32[]{:S(2)}, u32[]{:S(2)}) collective-permute-start(bf16[512,1024]{0,1:T(8,128)(2,1)} %get-tuple-element.159), channel_id=1, source_target_pairs={{0,1},{1,0},{2,3},{3,2},{4,5},{5,4},{6,7},{7,6},{8,9},{9,8},{10,11... | collective-permute-start | bytes 3145736 | tf_op jit(solution)/shard_map/ppermute | solution.py:426
  352.6 81.8 %collective-permute-start.12 = (bf16[512,1024]{0,1:T(8,128)(2,1)}, bf16[512,1024]{0,1:T(8,128)(2,1)}, u32[]{:S(2)}, u32[]{:S(2)}) collective-permute-start(bf16[512,1024]{0,1:T(8,128)(2,1)} %get-tuple-element.158), channel_id=1, source_target_pairs={{0,1},{1,0},{2,3},{3,2},{4,5},{5,4},{6,7},{7,6},{8,9},{9,8},{10,11... | collective-permute-start | bytes 3145736 | tf_op jit(solution)/shard_map/ppermute | solution.py:426
  432.3 25.3 %collective-permute-start.14 = (bf16[512,1024]{0,1:T(8,128)(2,1)S(1)}, bf16[512,1024]{0,1:T(8,128)(2,1)S(1)}, u32[]{:S(2)}, u32[]{:S(2)}) collective-permute-start(bf16[512,1024]{0,1:T(8,128)(2,1)S(1)} %add_convert_fusion.2), channel_id=1, source_target_pairs={{0,2},{1,3},{2,0},{3,1},{4,6},{5,7},{6,4},{7,5},{8,10},{9,11},{10,... | collective-permute-start | bytes 3145736 | tf_op jit(solution)/shard_map/ppermute | solution.py:426
  434.3 23.3 %copy-start.55 = (bf16[2048,1286]{1,0:T(8,128)(2,1)}, bf16[2048,1286]{1,0:T(8,128)(2,1)S(1)}, u32[]{:S(2)}) copy-start(bf16[2048,1286]{1,0:T(8,128)(2,1)S(1)} %convert_dynamic-update-slice_fusion) | copy-start | bytes 15802372
  485.5 4.1 collective-permute-start.16
  485.5 11.1 %collective-permute-start.15 = (bf16[512,1024]{0,1:T(8,128)(2,1)}, bf16[512,1024]{0,1:T(8,128)(2,1)S(1)}, u32[]{:S(2)}, u32[]{:S(2)}) collective-permute-start(bf16[512,1024]{0,1:T(8,128)(2,1)} %get-tuple-element.156), channel_id=1, source_target_pairs={{0,1},{1,0},{2,3},{3,2},{4,5},{5,4},{6,7},{7,6},{8,9},{9,8},{10,11... | collective-permute-start | bytes 3145736 | tf_op jit(solution)/shard_map/ppermute | solution.py:426
  491.0 25.5 %collective-permute-start.17 = (bf16[512,1024]{0,1:T(8,128)(2,1)}, bf16[512,1024]{0,1:T(8,128)(2,1)}, u32[]{:S(2)}, u32[]{:S(2)}) collective-permute-start(bf16[512,1024]{0,1:T(8,128)(2,1)} %add_convert_fusion), channel_id=1, source_target_pairs={{0,2},{1,3},{2,0},{3,1},{4,6},{5,7},{6,4},{7,5},{8,10},{9,11},{10,... | collective-permute-start | bytes 3145736 | tf_op jit(solution)/shard_map/ppermute | solution.py:426
  491.8 24.7 %copy-start.25 = (bf16[512,1024]{0,1:T(8,128)(2,1)S(1)}, bf16[512,1024]{0,1:T(8,128)(2,1)}, u32[]{:S(2)}) copy-start(bf16[512,1024]{0,1:T(8,128)(2,1)} %copy-done.23) | copy-start | bytes 3145732
  491.8 24.7 %copy-start.58 = (f32[1024]{0:T(1024)S(1)}, f32[1024]{0:T(1024)}, u32[]{:S(2)}) copy-start(f32[1024]{0:T(1024)} %param.18) | copy-start | bytes 12292
  491.9 24.7 %copy-start.60 = (f32[512]{0:T(512)S(1)}, f32[512]{0:T(512)}, u32[]{:S(2)}) copy-start(f32[512]{0:T(512)} %copy-done.59) | copy-start | bytes 6148
  493.2 23.3 %copy-start.44 = (f32[128,2048]{1,0:T(8,128)}, f32[128,2048]{1,0:T(8,128)S(1)}, u32[]{:S(2)}) copy-start(f32[128,2048]{1,0:T(8,128)S(1)} %convert_element_type.200) | copy-start | bytes 3145732
  493.3 26.0 %copy-start.63 = (f32[1024]{0:T(1024)S(1)}, f32[1024]{0:T(1024)}, u32[]{:S(2)}) copy-start(f32[1024]{0:T(1024)} %get-tuple-element.143) | copy-start | bytes 12292
  496.6 41.5 %copy-start.62 = (f32[512]{0:T(512)S(1)}, f32[512]{0:T(512)}, u32[]{:S(2)}) copy-start(f32[512]{0:T(512)} %copy-done.61) | copy-start | bytes 6148
  496.6 20.0 %copy-start.42 = (bf16[512,1024]{0,1:T(8,128)(2,1)}, bf16[512,1024]{0,1:T(8,128)(2,1)S(1)}, u32[]{:S(2)}) copy-start(bf16[512,1024]{0,1:T(8,128)(2,1)S(1)} %collective-permute-done.15) | copy-start | bytes 3145732
  519.3 32.0 %copy-start.33 = (f32[512,1024]{0,1:T(8,128)S(1)}, f32[512,1024]{0,1:T(8,128)}, u32[]{:S(2)}) copy-start(f32[512,1024]{0,1:T(8,128)} %get-tuple-element.148) | copy-start | bytes 6291460
  519.4 3.8 collective-permute-start.18
  523.2 12.3 %collective-permute-start.19 = (f32[4626]{0:T(1024)S(1)}, f32[4626]{0:T(1024)S(1)}, u32[]{:S(2)}, u32[]{:S(2)}) collective-permute-start(f32[4626]{0:T(1024)S(1)} %add.176), channel_id=1, source_target_pairs={{0,8},{4,12},{8,0},{12,4},{16,24},{20,28},{24,16},{28,20},{1,9},{5... | collective-permute-start | bytes 55520 | tf_op jit(solution)/shard_map/ppermute | solution.py:426
  535.5 5.9 %collective-permute-start.20 = (f32[4626]{0:T(1024)S(1)}, f32[4626]{0:T(1024)S(1)}, u32[]{:S(2)}, u32[]{:S(2)}) collective-permute-start(f32[4626]{0:T(1024)S(1)} %add.177), channel_id=1, source_target_pairs={{0,16},{4,20},{8,24},{12,28},{16,0},{20,4},{24,8},{28,12},{1,17},{... | collective-permute-start | bytes 55520 | tf_op jit(solution)/shard_map/ppermute | solution.py:426
  541.4 15.9 %collective-permute-start.21 = (f32[3072]{0:T(1024)S(1)}, f32[3072]{0:T(1024)}, u32[]{:S(2)}, u32[]{:S(2)}) collective-permute-start(f32[3072]{0:T(1024)S(1)} %slice.184), channel_id=1, source_target_pairs={{0,1},{1,0},{2,3},{3,2},{4,5},{5,4},{6,7},{7,6},{8,9},{9,8},{10,11... | collective-permute-start | bytes 36872 | tf_op jit(solution)/shard_map/ppermute | solution.py:426
  551.3 8.2 %collective-permute-start.23 = (f32[128,512]{0,1:T(8,128)}, f32[128,512]{0,1:T(8,128)}, u32[]{:S(2)}, u32[]{:S(2)}) collective-permute-start(f32[128,512]{0,1:T(8,128)} %slice_convert_fusion), channel_id=1, source_target_pairs={{0,1},{1,0},{2,3},{3,2},{4,5},{5,4},{6,7},{7,6},{8,9},{9,8},{10,11... | collective-permute-start | bytes 786440 | tf_op jit(solution)/shard_map/ppermute | solution.py:426
  558.0 4.3 collective-permute-start.22
  560.5 8.5 %collective-permute-start.24 = (f32[128,512]{0,1:T(8,128)S(1)}, f32[128,512]{0,1:T(8,128)S(1)}, u32[]{:S(2)}, u32[]{:S(2)}) collective-permute-start(f32[128,512]{0,1:T(8,128)S(1)} %fusion.44), channel_id=1, source_target_pairs={{0,2},{1,3},{2,0},{3,1},{4,6},{5,7},{6,4},{7,5},{8,10},{9,11},{10,... | collective-permute-start | bytes 786440 | tf_op jit(solution)/shard_map/ppermute | solution.py:426
  (62 other events, 304.1 us)
Sparse Core Ops, SparseCore 0:
  11.9 62.8 all-gather.4
  76.9 71.5 all-gather.6
  197.0 31.8 all-gather.8
  286.6 34.4 all-gather.10
  334.0 88.0 reduce-scatter.4
  474.2 75.1 reduce-scatter.6
